TPU v7x, 256 devices: a whole 4x4x8 slice. The times are simulated.
256 devices in a mesh: row: 16 (over z, core), col: 16 (over x, y).
Axes of the slice: x: 4, y: 4, z: 8, core: 2. Of those that a mesh axis runs over, the one named last changes fastest.
Arguments:
- tokens: bfloat16 [2048, 3072], P('col', 'row'), may hold values from -6 to 6
- gate_weight: bfloat16 [3072, 8192], P('row', 'col'), may hold values from -0.109375 to 0.109375
- up_weight: bfloat16 [3072, 8192], P('row', 'col'), may hold values from -0.109375 to 0.109375
- down_weight: bfloat16 [8192, 3072], P('col', 'row'), may hold values from -0.0625 to 0.0625
- cotangent: bfloat16 [2048, 3072], P('col', 'row'), may hold values from -6 to 6
Outputs:
- output: bfloat16 [2048, 3072], P('col', 'row')
- grad_tokens: bfloat16 [2048, 3072], P('col', 'row')
- grad_gate: bfloat16 [3072, 8192], P('row', 'col')
- grad_up: bfloat16 [3072, 8192], P('row', 'col')
- grad_down: bfloat16 [8192, 3072], P('col', 'row')
All inputs are finite; a program needn't handle non-finite values.
Results may differ from a plain program's by a relative error of at most 0.005.
Values may be sent and summed in bfloat16 or wider, within the bound.
A program may use at most 64 MiB of HBM per device.

v0:
```python
import jax
import jax.numpy as jnp
from jax import lax
from jax.sharding import PartitionSpec as P


def right_product(left, right):
    return lax.dot_general(
        left, right, (((1,), (1,)), ((), ())), preferred_element_type=jnp.float32
    )


def token_product(left, right):
    return lax.dot_general(
        left, right, (((0,), (0,)), ((), ())), preferred_element_type=jnp.float32
    )


def body(tokens, gate_weight, up_weight, down_weight, cotangent):
    all_tokens, all_cotangent = (
        lax.all_gather(tokens, "col", axis=0, tiled=True),
        lax.all_gather(cotangent, "col", axis=0, tiled=True),
    )
    width = gate_weight.shape[1]
    block = all_tokens
    both_rows = lax.psum_scatter(
        jnp.concatenate(
            [
                jnp.dot(block, gate_weight, preferred_element_type=jnp.float32),
                jnp.dot(block, up_weight, preferred_element_type=jnp.float32),
            ],
            axis=1,
        ),
        "row",
        scatter_dimension=0,
        tiled=True,
    )
    gate = both_rows[:, :width]
    up = both_rows[:, width:]
    hidden = (jax.nn.silu(gate) * up).astype(jnp.bfloat16)
    all_hidden = lax.all_gather(hidden, "row", axis=0, tiled=True)
    block = all_hidden
    output = lax.psum_scatter(
        jnp.dot(block, down_weight, preferred_element_type=jnp.float32),
        "col",
        scatter_dimension=0,
        tiled=True,
    ).astype(jnp.bfloat16)
    block = all_cotangent
    grad_hidden = lax.psum_scatter(
        right_product(block, down_weight), "row", scatter_dimension=0, tiled=True
    )
    sigma = jax.nn.sigmoid(gate)
    grad_up_act = (grad_hidden * (gate * sigma)).astype(jnp.bfloat16)
    grad_gate_act = (grad_hidden * up * sigma * (1.0 + gate * (1.0 - sigma))).astype(jnp.bfloat16)
    all_grad_gate, all_grad_up = (
        lax.all_gather(grad_gate_act, "row", axis=0, tiled=True),
        lax.all_gather(grad_up_act, "row", axis=0, tiled=True),
    )
    grad_down = token_product(all_hidden, all_cotangent).astype(jnp.bfloat16)
    grad_gate = token_product(all_tokens, all_grad_gate).astype(jnp.bfloat16)
    grad_up = token_product(all_tokens, all_grad_up).astype(jnp.bfloat16)
    grad_tokens = lax.psum_scatter(
        right_product(all_grad_gate, gate_weight) + right_product(all_grad_up, up_weight),
        "col",
        scatter_dimension=0,
        tiled=True,
    ).astype(jnp.bfloat16)
    return (output, grad_tokens, grad_gate, grad_up, grad_down)


def solution(mesh):
    return jax.shard_map(
        body,
        mesh=mesh,
        in_specs=(
            P("col", "row"),
            P("row", "col"),
            P("row", "col"),
            P("col", "row"),
            P("col", "row"),
        ),
        out_specs=(
            P("col", "row"),
            P("col", "row"),
            P("row", "col"),
            P("row", "col"),
            P("col", "row"),
        ),
        check_vma=False,
    )
```

profile of v0, /device:TPU:1, one launch (start us, length us, event | category | flops | bytes accessed | tf_op | source)
XLA Modules:
  0.0 468.9 jit_solution(9995470636479664625)
XLA Ops:
  7.2 21.6 %all_gather.17 = bf16[2048,192]{0,1:T(8,128)(2,1)S(1)} all-gather(bf16[128,192]{0,1:T(8,128)(2,1)} %param.9), channel_id=1, replica_groups=mesh['row'=16,'col'=16] {'col'}, dimensions={0}, use_global_device_ids=true | all-gather | bytes 835584 | tf_op jit(solution)/shard_map/all_gather | solution.py:22
  28.8 3.6 fusion.5
  32.5 0.0 reduce-scatter.5.cloned.1.call-start
  32.6 0.7 copy-done.4
  33.3 19.2 %all_gather.15 = bf16[2048,192]{0,1:T(8,128)(2,1)S(1)} all-gather(bf16[128,192]{0,1:T(8,128)(2,1)S(1)} %copy-done.4), channel_id=1, replica_groups=mesh['row'=16,'col'=16] {'col'}, dimensions={0}, use_global_device_ids=true | all-gather | bytes 835584 | tf_op jit(solution)/shard_map/all_gather | solution.py:21
  52.5 0.8 fusion.3
  53.3 0.2 copy-done.3
  53.5 0.8 fusion.4
  54.2 3.8 pad_maximum_fusion
  58.0 0.0 all-gather.6.cloned.1.call-start
  58.1 40.4 %reduce-scatter.9.cloned.1.call-done = f32[128,512]{0,1:T(8,128)} async-done(((f32[2048,512]{0,1:T(8,128)}), f32[128,512]{0,1:T(8,128)}) %reduce-scatter.9.cloned.1.call-update) | async-done | bytes 262160 | tf_op jit(solution)/shard_map/reduce_scatter | solution.py:50
  98.5 71.4 %reduce-scatter.5.cloned.1.call-done = f32[128,1024]{0,1:T(8,128)} async-done(((f32[2048,1024]{0,1:T(8,128)}), f32[128,1024]{0,1:T(8,128)}) %reduce-scatter.5.cloned.1.call-update) | async-done | bytes 524304 | tf_op jit(solution)/shard_map/reduce_scatter | solution.py:26
  169.9 2.0 multiply_convert_fusion
  171.9 0.0 all-gather.8.cloned.1.call-start
  172.0 0.5 all-gather.8.cloned.1.call-update
  172.5 0.5 all-gather.4.cloned.1.call-update
  173.1 0.0 reduce-scatter.11.cloned.1.call-start
  173.1 42.2 %all-gather.6.cloned.1.call-done = bf16[2048,512]{0,1:T(8,128)(2,1)} async-done(((bf16[128,512]{0,1:T(8,128)(2,1)}), bf16[2048,512]{0,1:T(8,128)(2,1)}) %all-gather.6.cloned.1.call-update) | async-done | bytes 2097168 | tf_op jit(solution)/shard_map/all_gather | solution.py:57
  215.3 2.2 fusion.7
  217.5 40.1 %all-gather.8.cloned.1.call-done = bf16[2048,512]{0,1:T(8,128)(2,1)} async-done(((bf16[128,512]{0,1:T(8,128)(2,1)}), bf16[2048,512]{0,1:T(8,128)(2,1)}) %all-gather.8.cloned.1.call-update) | async-done | bytes 2097168 | tf_op jit(solution)/shard_map/all_gather | solution.py:58
  257.6 3.4 convolution_add_fusion
  261.1 0.0 reduce-scatter.7.cloned.1.call-start
  261.1 38.8 %all-gather.4.cloned.1.call-done = bf16[2048,512]{0,1:T(8,128)(2,1)} async-done(((bf16[128,512]{0,1:T(8,128)(2,1)}), bf16[2048,512]{0,1:T(8,128)(2,1)}) %all-gather.4.cloned.1.call-update) | async-done | bytes 2097168 | tf_op jit(solution)/shard_map/all_gather | solution.py:41
  300.0 3.4 fusion.6
  303.4 3.3 fusion
  306.7 1.5 fusion.1
  308.2 0.1 copy-done.1
  308.3 1.5 convolution_convert_fusion
  309.8 69.3 %reduce-scatter.11.cloned.1.call-done = f32[128,192]{0,1:T(8,128)} async-done(((f32[2048,192]{0,1:T(8,128)}), f32[128,192]{0,1:T(8,128)}) %reduce-scatter.11.cloned.1.call-update) | async-done | bytes 98320 | tf_op jit(solution)/shard_map/reduce_scatter | solution.py:63
  379.1 1.5 convert_element_type.34
  380.6 79.9 %reduce-scatter.7.cloned.1.call-done = f32[128,192]{0,1:T(8,128)} async-done(((f32[2048,192]{0,1:T(8,128)}), f32[128,192]{0,1:T(8,128)}) %reduce-scatter.7.cloned.1.call-update) | async-done | bytes 98320 | tf_op jit(solution)/shard_map/reduce_scatter | solution.py:43
  460.6 1.5 convert_element_type.31
  (14 shorter events, 0.2 us)
Async XLA Ops:
  7.2 45.4 %copy-start = (bf16[192,512]{1,0:T(8,128)(2,1)S(1)}, bf16[192,512]{1,0:T(8,128)(2,1)}, u32[]{:S(2)}) copy-start(bf16[192,512]{1,0:T(8,128)(2,1)} %param.6) | copy-start | bytes 589828
  7.2 91.3 %reduce-scatter.9.cloned.1.call-start = ((), (), s32[]{:S(2)}) async-start(), calls=%async_computation.7 | async-start | bytes 4456448 | tf_op jit(solution)/shard_map/reduce_scatter | solution.py:50
  32.5 0.8 copy-start.4
  32.5 137.4 %reduce-scatter.5.cloned.1.call-start = ((), (), s32[]{:S(2)}) async-start(), calls=%async_computation.4 | async-start | bytes 8912896 | tf_op jit(solution)/shard_map/reduce_scatter | solution.py:26
  52.5 0.9 copy-start.3
  58.0 157.3 %all-gather.6.cloned.1.call-start = ((), (), s32[]{:S(2)}) async-start(), calls=%async_computation.8 | async-start | bytes 2228224 | tf_op jit(solution)/shard_map/all_gather | solution.py:57
  171.9 85.7 %all-gather.8.cloned.1.call-start = ((), (), s32[]{:S(2)}) async-start(), calls=%async_computation.9 | async-start | bytes 2228224 | tf_op jit(solution)/shard_map/all_gather | solution.py:58
  172.5 127.5 %all-gather.4.cloned.1.call-start = ((), (), s32[]{:S(2)}) async-start(), calls=%async_computation.5 | async-start | bytes 2228224 | tf_op jit(solution)/shard_map/all_gather | solution.py:41
  173.1 206.0 %reduce-scatter.11.cloned.1.call-start = ((), (), s32[]{:S(2)}) async-start(), calls=%async_computation.10 | async-start | bytes 1671168 | tf_op jit(solution)/shard_map/reduce_scatter | solution.py:63
  261.1 199.5 %reduce-scatter.7.cloned.1.call-start = ((), (), s32[]{:S(2)}) async-start(), calls=%async_computation.6 | async-start | bytes 1671168 | tf_op jit(solution)/shard_map/reduce_scatter | solution.py:43
  303.4 3.3 copy-start.2
  306.7 1.6 copy-start.1
Sparse Core Ops, SparseCore 0:
  32.6 65.8 reduce-scatter.8
  101.0 68.8 reduce-scatter.4
  172.2 43.0 all-gather.5
  217.5 40.0 all-gather.7
  259.8 40.0 all-gather.3
  303.3 75.7 reduce-scatter.10
  382.6 77.8 reduce-scatter.6
where the time goes:
time: 470 us; the launch traced here: 469 us
  waiting for transfers between devices  383 us (81%)
  blocking collectives  40.8 us (9%)
  matrix products  20.5 us (4%)
  between operations  14.2 us (3%)
  other arithmetic  8.81 us (2%)
    reduce_scatter x1, waiting for transfers between devices, body(): lax.psum_scatter(jnp.dot(block, down_weight, preferred_element_type=jnp.f...  79.9 us
    reduce_scatter x1, waiting for transfers between devices, body(): lax.psum_scatter(jnp.concatenate([jnp.dot(block, gate_weight, preferred_e...  71.4 us
    reduce_scatter x1, waiting for transfers between devices, body(): lax.psum_scatter(right_product(all_grad_gate, gate_weight) + right_produc...  69.3 us
    all_gather x1, waiting for transfers between devices, body(): lax.all_gather(grad_gate_act, 'row', axis=0, tiled=True)  42.2 us
    reduce_scatter x1, waiting for transfers between devices, body(): lax.psum_scatter(right_product(block, down_weight), 'row', scatter_dimens...  40.4 us
    all_gather x1, waiting for transfers between devices, body(): lax.all_gather(grad_up_act, 'row', axis=0, tiled=True)  40.1 us
    all_gather x1, waiting for transfers between devices, body(): all_hidden = lax.all_gather(hidden, 'row', axis=0, tiled=True)  38.8 us
    all_gather x1, blocking collectives, body(): lax.all_gather(cotangent, 'col', axis=0, tiled=True)  21.6 us
  transfers between devices with their start and end apart: 7, of which 7 were waited for; matrix products, arithmetic and copies ran while one was open for 5% of the time, Pallas kernels for 0%

commit v1 on v0

v1 whole, which is shorter than its diff:
```python
import jax
import jax.numpy as jnp
from jax import lax
from jax.experimental import pallas as pl
from jax.experimental.pallas import tpu as pltpu
from jax.sharding import PartitionSpec as P

MESH = pl.DeviceIdType.MESH
F32 = jnp.float32
BF16 = jnp.bfloat16

ORDER = (4, 3, 5, 2, 6, 1, 7, 0)
PIECE = 16
BLOCK = 256
HALF = 128
RIGHTWARD = (7, 6, 4, 2, 0)
LEFTWARD = (7, 5, 3, 1, 0)


def dot(a, b, ca, cb):
    return lax.dot_general(a, b, (((ca,), (cb,)), ((), ())), preferred_element_type=F32)


def kernel(
    tok, gw, uw, dw, cot,
    out, gt, gg, gu, gd,
    X, W, WD, WT, sent, got, part, final, H,
    S, SR, T, RX, U, UB, RY, acc, accd, gsend, gdsend,
    w_s, w_r, ag_s, ag_r, fw_s, fw_r, rs_s, rs_r, ga_s, ga_r, sx_s, sx_r, xy_s, xy_r, gr_s, gr_r,
):
    row, col = lax.axis_index("row"), lax.axis_index("col")
    z, k = row // 2, row % 2
    x, y = col // 4, col % 4
    other = 1 - k
    sibling = (z * 2 + other, col)
    right = (lax.rem(z + 1, 8) * 2 + k, col)
    left = (lax.rem(z + 7, 8) * 2 + k, col)

    def xpeer(i):
        return (row, lax.rem(x + i, 4) * 4 + y)

    def ypeer(i):
        return (row, x * 4 + lax.rem(y + i, 4))

    def copy(src, dst, s, r, device):
        return pltpu.make_async_remote_copy(
            src_ref=src, dst_ref=dst, send_sem=s, recv_sem=r, device_id=device, device_id_type=MESH
        )

    started = {}

    def start(key, c):
        c.start()
        started[key] = c

    def arrive(*key):
        started[key].wait_recv()

    barrier = pltpu.get_barrier_semaphore()
    for device in [sibling, right, left] + [xpeer(i) for i in (1, 2, 3)] + [ypeer(i) for i in (1, 2, 3)]:
        pl.semaphore_signal(barrier, inc=1, device_id=device, device_id_type=MESH)

    for a, ref in enumerate((tok, cot)):
        for o, d in enumerate(ORDER):
            j = lax.rem(z + d, 8)
            X[a, k, x, y, o] = ref[pl.ds(pl.multiple_of(j * PIECE, PIECE), PIECE), :]
    pl.semaphore_wait(barrier, 9)

    def gather1(a, c):
        for cls, peer in ((0, xpeer), (1, ypeer)):
            o = 4 * c + 2 * cls
            ref = X.at[a, k, x, y, pl.ds(o, 2)]
            for i in (1, 2, 3):
                start(
                    ("gather", a, c, cls, 0, i),
                    copy(ref, ref, ag_s.at[a, c, cls, 0, i - 1], ag_r.at[a, c, cls, 0, i - 1], peer(i)),
                )

    def gather2(a, c):
        for cls, peer in ((0, ypeer), (1, xpeer)):
            o = 4 * c + 2 * cls
            for i in (1, 2, 3):
                arrive("gather", a, c, cls, 0, i)
            ref = X.at[a, k, :, y, pl.ds(o, 2)] if cls == 0 else X.at[a, k, x, :, pl.ds(o, 2)]
            for i in (1, 2, 3):
                start(
                    ("gather", a, c, cls, 1, i),
                    copy(ref, ref, ag_s.at[a, c, cls, 1, i - 1], ag_r.at[a, c, cls, 1, i - 1], peer(i)),
                )

    def gather3(a, c):
        for cls in range(2):
            for i in (1, 2, 3):
                arrive("gather", a, c, cls, 1, i)
        ref = X.at[a, k, :, :, pl.ds(4 * c, 4)]
        start(("pair", a, c), copy(ref, ref, fw_s.at[a, c], fw_r.at[a, c], sibling))

    def gather4(a, c):
        arrive("pair", a, c)

    gather1(0, 0)
    gather1(1, 0)
    gather1(0, 1)
    gather1(1, 1)

    mine = pl.ds(pl.multiple_of(k * BLOCK, BLOCK), BLOCK)
    theirs = pl.ds(pl.multiple_of(other * BLOCK, BLOCK), BLOCK)
    start(("weight", 0), copy(gw.at[:, theirs], W.at[0, k], w_s.at[0], w_r.at[0], sibling))
    start(("weight", 1), copy(uw.at[:, theirs], W.at[1, k], w_s.at[1], w_r.at[1], sibling))
    start(("weight", 2), copy(dw.at[theirs, :], WD.at[k], w_s.at[2], w_r.at[2], sibling))
    W[0, k] = gw[:, mine]
    W[1, k] = uw[:, mine]
    WD[k] = dw[mine, :]
    for dr in range(2):
        for a in range(3):
            got[a, dr, 0, pl.ds(HALF * (1 - dr), HALF), :] = jnp.zeros((HALF, BLOCK), BF16)

    gather2(0, 0)
    for i in range(3):
        arrive("weight", i)
    width = dw.shape[1]
    eye = (
        lax.broadcasted_iota(jnp.int32, (width, width), 0) == lax.broadcasted_iota(jnp.int32, (width, width), 1)
    ).astype(BF16)
    for h in range(2):
        WT[h] = dot(eye, WD[h], 1, 1).astype(BF16)
    gather3(0, 0)
    gather2(1, 0)
    gather2(0, 1)
    gather4(0, 0)

    def local(a, o, first, rows):
        total = None
        for h in range(2):
            block = X[a // 2, h, pl.ds(first, rows // 64), :, o].reshape(rows, width)
            p = dot(block, W[a, h] if a < 2 else WT[h], 1, 0)
            total = p if total is None else total + p
        return total

    def chain(a, dr, s, rows):
        return copy(
            sent.at[a, dr, s, rows],
            got.at[a, dr, s, rows],
            rs_s.at[a, dr, s],
            rs_r.at[a, dr, s],
            right if dr == 0 else left,
        )

    def half(dr):
        return pl.ds(HALF * dr, HALF)

    def step0(a):
        for dr in range(2):
            sent[a, dr, 0, half(dr), :] = local(a, 0, 2 * dr, HALF).astype(BF16)
            start(("chain", a, dr, 0), chain(a, dr, 0, half(dr)))

    def step(a, s):
        for dr in range(2):
            part[dr] = local(a, 2 * s - 1 + dr, 0, BLOCK)
        for dr in range(2):
            arrive("chain", a, dr, s - 1)
            sent[a, dr, s] = (part[dr] + got[a, dr, s - 1].astype(F32)).astype(BF16)
            start(("chain", a, dr, s), chain(a, dr, s, pl.ds(0, BLOCK)))

    def finish(a):
        final[a] = local(a, 7, 0, BLOCK)
        for dr in range(2):
            arrive("chain", a, dr, 3)
        final[a] += got[a, 0, 3].astype(F32) + got[a, 1, 3].astype(F32)

    step0(0)
    step0(1)
    gather3(1, 0)
    gather2(1, 1)
    gather3(0, 1)
    gather4(1, 0)
    step0(2)
    gather3(1, 1)
    step(0, 1)
    step(1, 1)
    step(2, 1)
    gather4(0, 1)
    step(0, 2)
    step(1, 2)
    gather4(1, 1)
    step(2, 2)
    for a in range(3):
        step(a, 3)

    def relay(m, dr, s):
        places = RIGHTWARD if dr == 0 else LEFTWARD
        rows = half(dr) if s == 3 else pl.ds(0, BLOCK)
        lo, n = (0, 1) if m == 0 else (1, 2)
        return copy(
            H.at[pl.ds(lo, n), places[s], rows],
            H.at[pl.ds(lo, n), places[s + 1], rows],
            ga_s.at[m, dr, s],
            ga_r.at[m, dr, s],
            right if dr == 0 else left,
        )

    def relay_step(m, s):
        for dr in range(2):
            if s > 0:
                arrive("relay", m, dr, s - 1)
            start(("relay", m, dr, s), relay(m, dr, s))

    def relay_end(m):
        for dr in range(2):
            arrive("relay", m, dr, 3)

    finish(0)
    finish(1)
    gate, up = final[0], final[1]
    sigma = jax.nn.sigmoid(gate)
    H[0, 7] = ((gate * sigma) * up).astype(BF16)
    relay_step(0, 0)
    finish(2)
    gate, up, gh = final[0], final[1], final[2]
    sigma = jax.nn.sigmoid(gate)
    H[1, 7] = (gh * up * sigma * (1.0 + gate * (1.0 - sigma))).astype(BF16)
    H[2, 7] = (gh * (gate * sigma)).astype(BF16)
    relay_step(1, 0)

    def products(i, c):
        def body(o, carry):
            place = 4 * c + o
            for h in range(2):
                if i == 0:
                    p = dot(H[0, place], WD[h], 1, 0)
                else:
                    p = dot(H[1, place], W[0, h], 1, 1) + dot(H[2, place], W[1, h], 1, 1)
                S[i, c, h, :, :, o] = p.reshape(4, 4, PIECE, width)
            return carry

        lax.fori_loop(0, 4, body, 0)
        start(("cores", i, c), cores(i, c))

    def cores(i, c):
        return copy(S.at[i, c, other], SR.at[i, c], sx_s.at[i, c], sx_r.at[i, c], sibling)

    def scatter(i, c, cls, phase, n):
        if phase == 0:
            if cls == 0:
                src, peer = T.at[i, c, lax.rem(x + n, 4), :, pl.ds(0, 2)], xpeer(n)
            else:
                src, peer = T.at[i, c, :, lax.rem(y + n, 4), pl.ds(2, 2)], ypeer(n)
            dst = RX.at[i, c, cls, n - 1]
        else:
            if cls == 0:
                src, peer = UB.at[i, c, 0, lax.rem(y + n, 4)], ypeer(n)
            else:
                src, peer = UB.at[i, c, 1, lax.rem(x + n, 4)], xpeer(n)
            dst = RY.at[i, c, cls, n - 1]
        return copy(src, dst, xy_s.at[i, c, cls, phase, n - 1], xy_r.at[i, c, cls, phase, n - 1], peer)

    def scatter1(i, c):
        arrive("cores", i, c)

        def body(v, carry):
            T[i, c, v] = S[i, c, k, v] + SR[i, c, v]
            return carry

        lax.fori_loop(0, 4, body, 0)
        for cls in range(2):
            for n in (1, 2, 3):
                start(("scatter", i, c, cls, 0, n), scatter(i, c, cls, 0, n))

    def scatter2(i, c):
        for cls in range(2):
            if cls == 0:
                total = S[i, c, k, x, :, 0:2] + SR[i, c, x, :, 0:2]
            else:
                total = S[i, c, k, :, y, 2:4] + SR[i, c, :, y, 2:4]
            for n in (1, 2, 3):
                arrive("scatter", i, c, cls, 0, n)
                total = total + RX[i, c, cls, n - 1]
            U[i, c, cls] = total
            UB[i, c, cls] = total
            for n in (1, 2, 3):
                start(("scatter", i, c, cls, 1, n), scatter(i, c, cls, 1, n))

    def scatter3(i, c):
        ref = (out, gt)[i]
        for cls in range(2):
            total = U[i, c, cls, y if cls == 0 else x]
            for n in (1, 2, 3):
                arrive("scatter", i, c, cls, 1, n)
                total = total + RY[i, c, cls, n - 1]
            for p in range(2):
                j = lax.rem(z + ORDER[4 * c + 2 * cls + p], 8)
                ref[pl.ds(pl.multiple_of(j * PIECE, PIECE), PIECE), :] = total[p].astype(BF16)

    def grad(n):
        def body(o, carry):
            for h in range(2):
                if n == 2:
                    p = dot(H[0, o], X[1, h, :, :, o].reshape(BLOCK, width), 0, 0)
                    accd[h] = jnp.where(o == 0, p, accd[h] + p)
                else:
                    p = dot(X[0, h, :, :, o].reshape(BLOCK, width), H[1 + n, o], 0, 0)
                    acc[n, h] = jnp.where(o == 0, p, acc[n, h] + p)
            return carry

        lax.fori_loop(0, 8, body, 0)
        if n == 2:
            gdsend[...] = accd[other].astype(BF16)
            gd[mine, :] = accd[k].astype(BF16)
        else:
            gsend[n] = acc[n, other].astype(BF16)
            (gg, gu)[n][:, mine] = acc[n, k].astype(BF16)
        start(("grad", n), grad_copy(n))

    def grad_copy(n):
        if n == 2:
            return copy(gdsend, gd.at[mine, :], gr_s.at[2], gr_r.at[2], sibling)
        return copy(gsend.at[n], (gg, gu)[n].at[:, mine], gr_s.at[n], gr_r.at[n], sibling)

    relay_step(0, 1)
    relay_step(1, 1)
    relay_step(0, 2)
    products(0, 1)
    relay_step(1, 2)
    products(1, 1)
    scatter1(0, 1)
    relay_step(0, 3)
    scatter1(1, 1)
    scatter2(0, 1)
    relay_step(1, 3)
    scatter2(1, 1)
    relay_end(0)
    products(0, 0)
    grad(2)
    scatter1(0, 0)
    relay_end(1)
    products(1, 0)
    scatter2(0, 0)
    scatter1(1, 0)
    grad(0)
    scatter2(1, 0)
    grad(1)
    scatter3(0, 1)
    scatter3(1, 1)
    scatter3(0, 0)
    scatter3(1, 0)
    for n in (2, 0, 1):
        arrive("grad", n)
    for c in started.values():
        c.wait_send()


def body(tokens, gate_weight, up_weight, down_weight, cotangent):
    n_tok, width = tokens.shape
    hidden = gate_weight.shape[1]
    vmem = pl.BlockSpec(memory_space=pltpu.VMEM)
    dma = pltpu.SemaphoreType.DMA
    V = pltpu.VMEM
    scratch = [
        V((2, 2, 4, 4, 8, PIECE, width), BF16),
        V((2, 2, width, BLOCK), BF16),
        V((2, BLOCK, width), BF16),
        V((2, width, BLOCK), BF16),
        V((3, 2, 4, BLOCK, BLOCK), BF16),
        V((3, 2, 4, BLOCK, BLOCK), BF16),
        V((2, BLOCK, BLOCK), F32),
        V((3, BLOCK, BLOCK), F32),
        V((3, 8, BLOCK, BLOCK), BF16),
        V((2, 2, 2, 4, 4, 4, PIECE, width), F32),
        V((2, 2, 4, 4, 4, PIECE, width), F32),
        V((2, 2, 4, 4, 4, PIECE, width), F32),
        V((2, 2, 2, 3, 4, 2, PIECE, width), F32),
        V((2, 2, 2, 4, 2, PIECE, width), F32),
        V((2, 2, 2, 4, 2, PIECE, width), F32),
        V((2, 2, 2, 3, 2, PIECE, width), F32),
        V((2, 2, width, BLOCK), F32),
        V((2, BLOCK, width), F32),
        V((2, width, BLOCK), BF16),
        V((BLOCK, width), BF16),
        dma((3,)), dma((3,)),
        dma((2, 2, 2, 2, 3)), dma((2, 2, 2, 2, 3)),
        dma((2, 2)), dma((2, 2)),
        dma((3, 2, 4)), dma((3, 2, 4)),
        dma((2, 2, 4)), dma((2, 2, 4)),
        dma((2, 2)), dma((2, 2)),
        dma((2, 2, 2, 2, 3)), dma((2, 2, 2, 2, 3)),
        dma((3,)), dma((3,)),
    ]
    return pl.pallas_call(
        kernel,
        out_shape=(
            jax.ShapeDtypeStruct((n_tok, width), BF16),
            jax.ShapeDtypeStruct((n_tok, width), BF16),
            jax.ShapeDtypeStruct((width, hidden), BF16),
            jax.ShapeDtypeStruct((width, hidden), BF16),
            jax.ShapeDtypeStruct((hidden, width), BF16),
        ),
        in_specs=[vmem] * 5,
        out_specs=(vmem,) * 5,
        scratch_shapes=scratch,
        name="feed_forward",
        compiler_params=pltpu.CompilerParams(
            collective_id=0, has_side_effects=True, vmem_limit_bytes=56 * 2**20
        ),
    )(tokens, gate_weight, up_weight, down_weight, cotangent)


def solution(mesh):
    return jax.shard_map(
        body,
        mesh=mesh,
        in_specs=(
            P("col", "row"),
            P("row", "col"),
            P("row", "col"),
            P("col", "row"),
            P("col", "row"),
        ),
        out_specs=(
            P("col", "row"),
            P("col", "row"),
            P("row", "col"),
            P("row", "col"),
            P("col", "row"),
        ),
        check_vma=False,
    )
```

time: 470 us -> 128 us (0.27)
  waiting for transfers between devices: 383 us -> 0 us
  Pallas kernels: 0 us -> 118 us
  blocking collectives: 40.8 us -> 0 us
  matrix products: 20.5 us -> 0 us
  between operations: 14.2 us -> 0.66 us
  other arithmetic: 8.81 us -> 0 us
  local copies, waits for them, and re-layouts: 0.96 us -> 9.72 us
    reduce_scatter x4 -> x0, waiting for transfers between devices: 261 us -> none  [the longest x1 79.9 us: body(): lax.psum_scatter(jnp.dot(block, down_weight, preferred_element_type=jnp.f...]
    all_gather x3 -> x0, waiting for transfers between devices: 121 us -> none  [the longest x1 42.2 us: body(): lax.all_gather(grad_gate_act, 'row', axis=0, tiled=True)]
    pallas_call x0 -> x1, Pallas kernels: none -> 118 us  [body(): pl.pallas_call(kernel, out_shape=(jax.ShapeDtypeStruct((n_tok, width), BF...]
    all_gather x2 -> x0, blocking collectives: 40.8 us -> none  [the longest x1 21.6 us: body(): lax.all_gather(cotangent, 'col', axis=0, tiled=True)]
    dot_general x9 -> x0, matrix products: 20.5 us -> none  [the longest x3 9.24 us: right_product(): lax.dot_general(left, right, (((1,), (1,)), ((), ())), preferred_element_...]
    convert_element_type x3 -> x0, other arithmetic: 5.01 us -> none  [the longest x1 1.98 us: body(): grad_up_act = (grad_hidden * (gate * sigma)).astype(jnp.bfloat16)]
  transfers between devices with their start and end apart: 7 -> 0, of which waited for: 7 -> 0; matrix products, arithmetic and copies ran while one was open for 5% -> 0% of each run, Pallas kernels for 0% -> 0%
where the time goes in v1:
time: 128 us
  Pallas kernels  118 us (92%)
  local copies, waits for them, and re-layouts  9.72 us (8%)
    pallas_call x1, Pallas kernels, body(): pl.pallas_call(kernel, out_shape=(jax.ShapeDtypeStruct((n_tok, width), BF...  118 us
    unnamed x13, local copies, waits for them, and re-layouts  5.62 us
    pallas_call x3, local copies, waits for them, and re-layouts, body(): pl.pallas_call(kernel, out_shape=(jax.ShapeDtypeStruct((n_tok, width), BF...  4.11 us

profile of v1, /device:TPU:1, one launch (start us, length us, event | category | flops | bytes accessed | tf_op | source)
XLA Modules:
  0.0 128.1 jit_solution(277902723912448397)
XLA Ops:
  0.6 0.0 copy-start
  0.6 1.6 %copy.10.tok = bf16[128,192]{1,0:T(8,128)(2,1)} copy(bf16[128,192]{0,1:T(8,128)(2,1)} %param.5) | data formatting | bytes 98304 | tf_op args[0]
  2.2 1.5 %copy.12.cot = bf16[128,192]{1,0:T(8,128)(2,1)} copy(bf16[128,192]{0,1:T(8,128)(2,1)} %param.9) | data formatting | bytes 98304 | tf_op args[4]
  3.7 0.0 copy-done
  3.7 0.8 copy.11.dw
  4.6 117.7 %feed_forward.1 = (bf16[128,192]{1,0:T(8,128)(2,1)}, bf16[128,192]{1,0:T(8,128)(2,1)}, bf16[192,512]{1,0:T(8,128)(2,1)}, bf16[192,512]{1,0:T(8,128)(2,1)}, bf16[512,192]{1,0:T(8,128)(2,1)}) custom-call(bf16[128,192]{1,0:T(8,128)(2,1)} %copy.10.tok, bf16[192,512]{1,0:T(8,128)(2,1)} %gw.1, bf16[192,512]{1,0:T(8,128)(2,1)} %uw.1, bf16[512,192]{1,0:T(8,128)(2,1)} %copy.11.dw, ...), custom_call_target="tpu_custom_call" | custom-call | tf_op jit(solution)/shard_map/feed_forward/pallas_call | solution.py:388
  122.3 0.0 copy-start.3
  122.3 1.6 %copy.13 = bf16[128,192]{0,1:T(8,128)(2,1)} copy(bf16[128,192]{1,0:T(8,128)(2,1)} %get-tuple-element.5) | data formatting | bytes 98304 | tf_op jit(solution)/shard_map/feed_forward/pallas_call | solution.py:388
  123.9 0.0 copy-done.3
  123.9 0.7 copy.14
  124.6 0.0 copy-start.2
  124.6 1.8 %copy.15 = bf16[512,192]{0,1:T(8,128)(2,1)} copy(bf16[512,192]{1,0:T(8,128)(2,1)} %get-tuple-element.9) | data formatting | bytes 393216 | tf_op jit(solution)/shard_map/feed_forward/pallas_call | solution.py:388
  126.4 0.0 copy-done.2
  126.4 0.0 copy-start.1
  126.4 0.7 copy.18
  127.1 0.3 copy-done.1
  127.4 0.7 copy.19
Async XLA Ops:
  0.6 3.1 %copy-start = (bf16[512,192]{0,1:T(8,128)(2,1)S(1)}, bf16[512,192]{0,1:T(8,128)(2,1)}, u32[]{:S(2)}) copy-start(bf16[512,192]{0,1:T(8,128)(2,1)} %param.8) | copy-start | bytes 589828
  122.3 1.6 %copy-start.3 = (bf16[128,192]{1,0:T(8,128)(2,1)S(1)}, bf16[128,192]{1,0:T(8,128)(2,1)}, u32[]{:S(2)}) copy-start(bf16[128,192]{1,0:T(8,128)(2,1)} %get-tuple-element.6) | copy-start | bytes 147460
  124.6 1.8 %copy-start.2 = (bf16[192,512]{1,0:T(8,128)(2,1)S(1)}, bf16[192,512]{1,0:T(8,128)(2,1)}, u32[]{:S(2)}) copy-start(bf16[192,512]{1,0:T(8,128)(2,1)} %get-tuple-element.17) | copy-start | bytes 589828
  126.4 1.0 copy-start.1

commit v2 on v0

v2 whole, which is shorter than its diff:
```python
import jax
import jax.numpy as jnp
from jax import lax
from jax.experimental import pallas as pl
from jax.experimental.pallas import tpu as pltpu
from jax.sharding import PartitionSpec as P

MESH = pl.DeviceIdType.MESH
F32 = jnp.float32
BF16 = jnp.bfloat16

ORDER = (4, 3, 5, 0, 2, 1, 6, 7)
PLACE = {d: o for o, d in enumerate(ORDER)}
PIECE = 16
BLOCK = 256
HALF = 128
RIGHTWARD = tuple(PLACE[d] for d in (0, 7, 6, 5, 4))
LEFTWARD = tuple(PLACE[d] for d in (0, 1, 2, 3, 4))
NEAR = ((0, 4, 2, 0, 16), (1, 6, 2, 0, 16))
FAR = ((0, 0, 2, 0, 16), (1, 2, 2, 0, 16))
MIDDLE = ((0, 1, 1, 0, 16), (1, 2, 2, 0, 16))
LAST = ((0, 0, 1, 0, 8), (1, 0, 1, 8, 8))
PARTS = {(0, 0): NEAR, (0, 1): FAR, (1, 0): NEAR, (1, 1): MIDDLE, (1, 2): LAST}


def dot(a, b, ca, cb):
    return lax.dot_general(a, b, (((ca,), (cb,)), ((), ())), preferred_element_type=F32)


def identity(n):
    rows = lax.broadcasted_iota(jnp.int32, (n, n), 0)
    return (rows == lax.broadcasted_iota(jnp.int32, (n, n), 1)).astype(BF16)


def kernel(
    tok, gw, uw, dw, cot,
    out, gt, gg, gu, gd,
    acts, weights, rows_in, X, W, sent, got, part, final, H,
    S, SR, T, RX, U, RY, acc, gsend, ggot, grads, rows_out, results,
    in_s, out_s, w_s, w_r, ag_s, ag_r, fw_s, fw_r, rs_s, rs_r, ga_s, ga_r, sx_s, sx_r, xy_s, xy_r, gr_s, gr_r,
):
    row, col = lax.axis_index("row"), lax.axis_index("col")
    z, k = row // 2, row % 2
    x, y = col // 4, col % 4
    other = 1 - k
    width = gw.shape[0]
    sibling = (z * 2 + other, col)
    right = (lax.rem(z + 1, 8) * 2 + k, col)
    left = (lax.rem(z + 7, 8) * 2 + k, col)
    xpeers = {i: (row, lax.rem(x + i, 4) * 4 + y) for i in (1, 2, 3)}
    ypeers = {i: (row, x * 4 + lax.rem(y + i, 4)) for i in (1, 2, 3)}
    peers = (xpeers, ypeers)

    def copy(src, dst, s, r, device):
        return pltpu.make_async_remote_copy(
            src_ref=src, dst_ref=dst, send_sem=s, recv_sem=r, device_id=device, device_id_type=MESH
        )

    started = {}

    def start(key, c):
        c.start()
        started[key] = c

    def arrive(*key):
        started[key].wait_recv()

    barrier = pltpu.get_barrier_semaphore()
    for device in [sibling, right, left, *xpeers.values(), *ypeers.values()]:
        pl.semaphore_signal(barrier, inc=1, device_id=device, device_id_type=MESH)

    loads = [
        pltpu.make_async_copy(src, dst, in_s.at[i])
        for i, (src, dst) in enumerate(
            ((tok, acts.at[0]), (cot, acts.at[1]), (gw, weights.at[0]), (uw, weights.at[1]), (dw, weights.at[2]))
        )
    ]
    for c in loads:
        c.start()

    def pieces(a):
        loads[a].wait()
        rows_in[a] = dot(identity(HALF), acts[a], 1, 1).astype(BF16)
        for o, d in enumerate(ORDER):
            j = lax.rem(z + d, 8)
            X[a, k, x, y, o] = rows_in[a, pl.ds(pl.multiple_of(j * PIECE, PIECE), PIECE), :]

    def gather1(a, c):
        for cls in range(2):
            ref = X.at[a, k, x, y, pl.ds(4 * c + 2 * cls, 2)]
            for i in (1, 2, 3):
                start(
                    ("gather", a, c, cls, 0, i),
                    copy(ref, ref, ag_s.at[a, c, cls, 0, i - 1], ag_r.at[a, c, cls, 0, i - 1], peers[cls][i]),
                )

    def gather2(a, c):
        for cls in range(2):
            places = pl.ds(4 * c + 2 * cls, 2)
            for i in (1, 2, 3):
                arrive("gather", a, c, cls, 0, i)
            ref = X.at[a, k, :, y, places] if cls == 0 else X.at[a, k, x, :, places]
            for i in (1, 2, 3):
                start(
                    ("gather", a, c, cls, 1, i),
                    copy(ref, ref, ag_s.at[a, c, cls, 1, i - 1], ag_r.at[a, c, cls, 1, i - 1], peers[1 - cls][i]),
                )

    def gather3(a, c):
        for cls in range(2):
            for i in (1, 2, 3):
                arrive("gather", a, c, cls, 1, i)
        ref = X.at[a, k, :, :, pl.ds(4 * c, 4)]
        start(("pair", a, c), copy(ref, ref, fw_s.at[a, c], fw_r.at[a, c], sibling))

    def gather4(a, c):
        arrive("pair", a, c)

    mine = pl.ds(pl.multiple_of(k * BLOCK, BLOCK), BLOCK)
    theirs = pl.ds(pl.multiple_of(other * BLOCK, BLOCK), BLOCK)

    def swap_weights():
        for i in range(3):
            loads[2 + i].wait()
            start(("weight", i), copy(weights.at[i, :, theirs], W.at[i, k], w_s.at[i], w_r.at[i], sibling))
        for i in range(3):
            W[i, k] = weights[i, :, mine]

    def local(a, o, first, rows):
        total = None
        for h in range(2):
            block = X[a // 2, h, pl.ds(first, rows // 64), :, o].reshape(rows, width)
            p = dot(block, W[a, h], 1, 0)
            total = p if total is None else total + p
        return total

    def half(dr):
        return pl.ds(HALF * dr, HALF)

    def chain(a, dr, s, rows):
        start(
            ("chain", a, dr, s),
            copy(
                sent.at[a, dr, s, rows],
                got.at[a, dr, s, rows],
                rs_s.at[a, dr, s],
                rs_r.at[a, dr, s],
                (right, left)[dr],
            ),
        )

    def step0(a):
        for dr in range(2):
            sent[a, dr, 0, half(dr), :] = local(a, PLACE[4], 2 * dr, HALF).astype(BF16)
            chain(a, dr, 0, half(dr))

    def step(a, s):
        for dr in range(2):
            part[dr] = local(a, PLACE[(4 - s, 4 + s)[dr]], 0, BLOCK)
        for dr in range(2):
            arrive("chain", a, dr, s - 1)
            if s == 1:
                sent[a, dr, s, half(dr), :] = (part[dr, half(dr), :] + got[a, dr, 0, half(dr), :].astype(F32)).astype(BF16)
                sent[a, dr, s, half(1 - dr), :] = part[dr, half(1 - dr), :].astype(BF16)
            else:
                sent[a, dr, s] = (part[dr] + got[a, dr, s - 1].astype(F32)).astype(BF16)
            chain(a, dr, s, pl.ds(0, BLOCK))

    def finish(a):
        final[a] = local(a, PLACE[0], 0, BLOCK)
        for dr in range(2):
            arrive("chain", a, dr, 3)
        final[a] += got[a, 0, 3].astype(F32) + got[a, 1, 3].astype(F32)

    def relay_step(m, s):
        lo, n = (0, 1) if m == 0 else (1, 2)
        for dr in range(2):
            places = (RIGHTWARD, LEFTWARD)[dr]
            rows = half(dr) if s == 3 else pl.ds(0, BLOCK)
            if s > 0:
                arrive("relay", m, dr, s - 1)
            start(
                ("relay", m, dr, s),
                copy(
                    H.at[pl.ds(lo, n), places[s], rows],
                    H.at[pl.ds(lo, n), places[s + 1], rows],
                    ga_s.at[m, dr, s],
                    ga_r.at[m, dr, s],
                    (right, left)[dr],
                ),
            )

    def relay_end(m):
        for dr in range(2):
            arrive("relay", m, dr, 3)

    def activate():
        gate, up = final[0], final[1]
        H[0, PLACE[0]] = ((gate * jax.nn.sigmoid(gate)) * up).astype(BF16)

    def activate_back():
        gate, up, gh = final[0], final[1], final[2]
        sigma = jax.nn.sigmoid(gate)
        H[1, PLACE[0]] = (gh * up * sigma * (1.0 + gate * (1.0 - sigma))).astype(BF16)
        H[2, PLACE[0]] = (gh * (gate * sigma)).astype(BF16)

    def products(i, g, lo, n):
        def body(o, carry):
            for h in range(2):
                if i == 0:
                    p = dot(H[0, o], W[2, h], 1, 1)
                else:
                    p = dot(H[1, o], W[0, h], 1, 1) + dot(H[2, o], W[1, h], 1, 1)
                S[i, h, :, :, o] = p.reshape(4, 4, PIECE, width)
            return carry

        if n == 1:
            body(lo, 0)
        else:
            lax.fori_loop(lo, lo + n, body, 0)
        span = pl.ds(lo, n)
        start(
            ("cores", i, g),
            copy(S.at[i, other, :, :, span], SR.at[i, :, :, span], sx_s.at[i, g], sx_r.at[i, g], sibling),
        )

    def scatter1(i, g):
        arrive("cores", i, g)
        for cls, lo, n, r, m in PARTS[i, g]:
            span, rows = pl.ds(lo, n), pl.ds(r, m)
            T[i, :, :, span, rows] = S[i, k, :, :, span, rows] + SR[i, :, :, span, rows]
            for q in (1, 2, 3):
                if cls == 0:
                    src = T.at[i, lax.rem(x + q, 4), :, span, rows]
                else:
                    src = T.at[i, :, lax.rem(y + q, 4), span, rows]
                start(
                    ("scatter", i, g, cls, 0, q),
                    copy(
                        src,
                        RX.at[i, q - 1, :, span, rows],
                        xy_s.at[i, g, cls, 0, q - 1],
                        xy_r.at[i, g, cls, 0, q - 1],
                        peers[cls][q],
                    ),
                )

    def scatter2(i, g):
        for cls, lo, n, r, m in PARTS[i, g]:
            span, rows = pl.ds(lo, n), pl.ds(r, m)
            total = T[i, x, :, span, rows] if cls == 0 else T[i, :, y, span, rows]
            for q in (1, 2, 3):
                arrive("scatter", i, g, cls, 0, q)
                total = total + RX[i, q - 1, :, span, rows]
            U[i, :, span, rows] = total
            for q in (1, 2, 3):
                at = lax.rem(y + q, 4) if cls == 0 else lax.rem(x + q, 4)
                start(
                    ("scatter", i, g, cls, 1, q),
                    copy(
                        U.at[i, at, span, rows],
                        RY.at[i, q - 1, span, rows],
                        xy_s.at[i, g, cls, 1, q - 1],
                        xy_r.at[i, g, cls, 1, q - 1],
                        peers[1 - cls][q],
                    ),
                )

    def scatter3(i, g):
        for cls, lo, n, r, m in PARTS[i, g]:
            span, rows = pl.ds(lo, n), pl.ds(r, m)
            total = U[i, y if cls == 0 else x, span, rows]
            for q in (1, 2, 3):
                arrive("scatter", i, g, cls, 1, q)
                total = total + RY[i, q - 1, span, rows]
            for p in range(n):
                j = lax.rem(z + ORDER[lo + p], 8)
                rows_out[i, pl.ds(pl.multiple_of(j * PIECE + r, 8), m), :] = total[p]

    stores = []

    def store(src, dst):
        c = pltpu.make_async_copy(src, dst, out_s.at[len(stores)])
        c.start()
        stores.append(c)

    def deliver(i):
        results[i] = dot(identity(width), rows_out[i].astype(BF16), 1, 1).astype(BF16)
        store(results.at[i], (out, gt)[i])

    def grad(n, lo, hi):
        a, b = ((0, 1), (0, 2), (1, 0))[n]

        def body(o, carry):
            for h in range(2):
                acc[n, h] += dot(X[a, h, :, :, o].reshape(BLOCK, width), H[b, o], 0, 0)
            return carry

        if hi - lo == 1:
            body(lo, 0)
        else:
            lax.fori_loop(lo, hi, body, 0)

    def grad_swap(n):
        gsend[n] = acc[n, other].astype(BF16)
        start(("grad", n), copy(gsend.at[n], ggot.at[n], gr_s.at[n], gr_r.at[n], sibling))
        grads[n, :, mine] = acc[n, k].astype(BF16)

    def grad_end(n):
        arrive("grad", n)
        grads[n, :, theirs] = ggot[n]
        store(grads.at[n], (gg, gu, gd)[n])

    pieces(0)
    pl.semaphore_wait(barrier, 9)
    gather1(0, 0)
    swap_weights()
    gather1(0, 1)
    pieces(1)
    gather2(0, 0)
    gather1(1, 0)
    acc[...] = jnp.zeros_like(acc)
    gather2(0, 1)
    gather3(0, 0)
    gather2(1, 0)
    gather1(1, 1)
    for i in range(3):
        arrive("weight", i)
    gather4(0, 0)
    step0(0)
    step0(1)
    gather3(0, 1)
    step(0, 1)
    step(1, 1)
    gather3(1, 0)
    gather2(1, 1)
    gather4(0, 1)
    step(0, 2)
    step(1, 2)
    gather4(1, 0)
    step0(2)
    gather3(1, 1)
    step(0, 3)
    step(1, 3)
    step(2, 1)
    gather4(1, 1)
    finish(0)
    finish(1)
    activate()
    relay_step(0, 0)
    step(2, 2)
    step(2, 3)
    relay_step(0, 1)
    finish(2)
    activate_back()
    relay_step(1, 0)
    relay_step(0, 2)
    products(0, 0, 4, 4)
    relay_step(1, 1)
    scatter1(0, 0)
    relay_step(0, 3)
    grad(2, 4, 8)
    relay_step(1, 2)
    products(1, 0, 4, 4)
    relay_end(0)
    products(0, 1, 0, 4)
    scatter1(1, 0)
    grad(2, 0, 4)
    relay_step(1, 3)
    products(1, 1, 1, 3)
    scatter2(0, 0)
    scatter1(0, 1)
    scatter2(1, 0)
    grad_swap(2)
    scatter1(1, 1)
    grad(0, 1, 8)
    grad(1, 1, 8)
    relay_end(1)
    products(1, 2, 0, 1)
    scatter2(0, 1)
    grad(0, 0, 1)
    grad_swap(0)
    scatter1(1, 2)
    scatter2(1, 1)
    grad(1, 0, 1)
    grad_swap(1)
    scatter3(0, 0)
    scatter3(0, 1)
    deliver(0)
    grad_end(2)
    scatter2(1, 2)
    scatter3(1, 0)
    grad_end(0)
    grad_end(1)
    scatter3(1, 1)
    scatter3(1, 2)
    deliver(1)
    for c in stores:
        c.wait()
    for c in started.values():
        c.wait_send()


def hand_over(*refs):
    sems = refs[10]
    copies = [pltpu.make_async_copy(refs[i], refs[5 + i], sems.at[i]) for i in range(5)]
    for c in copies:
        c.start()
    for c in copies:
        c.wait()


def body(tokens, gate_weight, up_weight, down_weight, cotangent):
    n_tok, width = tokens.shape
    hidden = gate_weight.shape[1]
    dma = pltpu.SemaphoreType.DMA
    V = pltpu.VMEM
    act = jax.ShapeDtypeStruct((width, n_tok), BF16)
    weight = jax.ShapeDtypeStruct((width, hidden), BF16)
    shapes = (act, act, weight, weight, weight)
    scratch = [
        V((2, width, n_tok), BF16),
        V((3, width, hidden), BF16),
        V((2, n_tok, width), BF16),
        V((2, 2, 4, 4, 8, PIECE, width), BF16),
        V((3, 2, width, BLOCK), BF16),
        V((3, 2, 4, BLOCK, BLOCK), BF16),
        V((3, 2, 4, BLOCK, BLOCK), BF16),
        V((2, BLOCK, BLOCK), F32),
        V((3, BLOCK, BLOCK), F32),
        V((3, 8, BLOCK, BLOCK), BF16),
        V((2, 2, 4, 4, 8, PIECE, width), F32),
        V((2, 4, 4, 8, PIECE, width), F32),
        V((2, 4, 4, 8, PIECE, width), F32),
        V((2, 3, 4, 8, PIECE, width), F32),
        V((2, 4, 8, PIECE, width), F32),
        V((2, 3, 8, PIECE, width), F32),
        V((3, 2, width, BLOCK), F32),
        V((3, width, BLOCK), BF16),
        V((3, width, BLOCK), BF16),
        V((3, width, hidden), BF16),
        V((2, n_tok, width), F32),
        V((2, width, n_tok), BF16),
        dma((5,)), dma((5,)),
        dma((3,)), dma((3,)),
        dma((2, 2, 2, 2, 3)), dma((2, 2, 2, 2, 3)),
        dma((2, 2)), dma((2, 2)),
        dma((3, 2, 4)), dma((3, 2, 4)),
        dma((2, 2, 4)), dma((2, 2, 4)),
        dma((2, 3)), dma((2, 3)),
        dma((2, 3, 2, 2, 3)), dma((2, 3, 2, 2, 3)),
        dma((3,)), dma((3,)),
    ]
    anywhere = pl.BlockSpec(memory_space=pl.ANY)
    held = pl.pallas_call(
        kernel,
        out_shape=shapes,
        in_specs=[anywhere] * 5,
        out_specs=(anywhere,) * 5,
        scratch_shapes=scratch,
        name="feed_forward",
        compiler_params=pltpu.CompilerParams(
            collective_id=0, has_side_effects=True, vmem_limit_bytes=56 * 2**20
        ),
    )(tokens.T, gate_weight, up_weight, down_weight.T, cotangent.T)
    results = pl.pallas_call(
        hand_over,
        out_shape=shapes,
        in_specs=[anywhere] * 5,
        out_specs=(anywhere,) * 5,
        scratch_shapes=[dma((5,))],
        name="hand_over",
        compiler_params=pltpu.CompilerParams(vmem_limit_bytes=60 * 2**20),
    )(*held)
    return results[0].T, results[1].T, results[2], results[3], results[4].T


def solution(mesh):
    return jax.shard_map(
        body,
        mesh=mesh,
        in_specs=(
            P("col", "row"),
            P("row", "col"),
            P("row", "col"),
            P("col", "row"),
            P("col", "row"),
        ),
        out_specs=(
            P("col", "row"),
            P("col", "row"),
            P("row", "col"),
            P("row", "col"),
            P("col", "row"),
        ),
        check_vma=False,
    )
```

time: 470 us -> 136 us (0.29)
  waiting for transfers between devices: 383 us -> 0 us
  Pallas kernels: 0 us -> 135 us
  blocking collectives: 40.8 us -> 0 us
  matrix products: 20.5 us -> 0 us
  between operations: 14.2 us -> 0.64 us
  other arithmetic: 8.81 us -> 0 us
    reduce_scatter x4 -> x0, waiting for transfers between devices: 261 us -> none  [the longest x1 79.9 us: body(): lax.psum_scatter(jnp.dot(block, down_weight, preferred_element_type=jnp.f...]
    pallas_call x0 -> x2, Pallas kernels: none -> 135 us  [the longest x1 113 us: body(): pl.pallas_call(kernel, out_shape=shapes, in_specs=[anywhere] * 5, out_spe...]
    all_gather x3 -> x0, waiting for transfers between devices: 121 us -> none  [the longest x1 42.2 us: body(): lax.all_gather(grad_gate_act, 'row', axis=0, tiled=True)]
    all_gather x2 -> x0, blocking collectives: 40.8 us -> none  [the longest x1 21.6 us: body(): lax.all_gather(cotangent, 'col', axis=0, tiled=True)]
    dot_general x9 -> x0, matrix products: 20.5 us -> none  [the longest x3 9.24 us: right_product(): lax.dot_general(left, right, (((1,), (1,)), ((), ())), preferred_element_...]
    convert_element_type x3 -> x0, other arithmetic: 5.01 us -> none  [the longest x1 1.98 us: body(): grad_up_act = (grad_hidden * (gate * sigma)).astype(jnp.bfloat16)]
  transfers between devices with their start and end apart: 7 -> 0, of which waited for: 7 -> 0; matrix products, arithmetic and copies ran while one was open for 5% -> 0% of each run, Pallas kernels for 0% -> 0%
where the time goes in v2:
time: 136 us; the launch traced here: 135 us
  Pallas kernels  135 us (99%)
    pallas_call x1, Pallas kernels, body(): pl.pallas_call(kernel, out_shape=shapes, in_specs=[anywhere] * 5, out_spe...  113 us
    pallas_call x1, Pallas kernels, body(): pl.pallas_call(hand_over, out_shape=shapes, in_specs=[anywhere] * 5, out_...  22 us

profile of v2, /device:TPU:1, one launch (start us, length us, event | category | flops | bytes accessed | tf_op | source)
XLA Modules:
  0.0 135.4 jit_solution(16532295942115990890)
XLA Ops:
  0.6 112.8 %feed_forward.1 = (bf16[192,128]{1,0:T(8,128)(2,1)}, bf16[192,128]{1,0:T(8,128)(2,1)}, bf16[192,512]{1,0:T(8,128)(2,1)}, bf16[192,512]{1,0:T(8,128)(2,1)}, bf16[192,512]{1,0:T(8,128)(2,1)}) custom-call(bf16[192,128]{1,0:T(8,128)(2,1)} %bitcast.7, bf16[192,512]{1,0:T(8,128)(2,1)} %gw.1, bf16[192,512]{1,0:T(8,128)(2,1)} %uw.1, bf16[192,512]{1,0:T(8,128)(2,1)} %bitcast.6, ...), custom_call_target="tpu_custom_call" | custom-call | tf_op jit(solution)/shard_map/feed_forward/pallas_call | solution.py:455
  113.4 22.0 %hand_over.1 = (bf16[192,128]{1,0:T(8,128)(2,1)}, bf16[192,128]{1,0:T(8,128)(2,1)}, bf16[192,512]{1,0:T(8,128)(2,1)}, bf16[192,512]{1,0:T(8,128)(2,1)}, bf16[192,512]{1,0:T(8,128)(2,1)}) custom-call(bf16[192,128]{1,0:T(8,128)(2,1)} %get-tuple-element.15.refs_0_, bf16[192,128]{1,0:T(8,128)(2,1)} %get-tuple-element.16.refs_1_, ...), custom_call_target="tpu_custom_call" | custom-call | tf_op jit(solution)/shard_map/hand_over/pallas_call | solution.py:466

commit v3 on v2

--- a/solution.py
+++ b/solution.py
@@ -12,14 +12,16 @@
 ORDER = (4, 3, 5, 0, 2, 1, 6, 7)
 PLACE = {d: o for o, d in enumerate(ORDER)}
 PIECE = 16
+LANES = 128
+TAIL = 64
 BLOCK = 256
 HALF = 128
 RIGHTWARD = tuple(PLACE[d] for d in (0, 7, 6, 5, 4))
 LEFTWARD = tuple(PLACE[d] for d in (0, 1, 2, 3, 4))
-NEAR = ((0, 4, 2, 0, 16), (1, 6, 2, 0, 16))
-FAR = ((0, 0, 2, 0, 16), (1, 2, 2, 0, 16))
-MIDDLE = ((0, 1, 1, 0, 16), (1, 2, 2, 0, 16))
-LAST = ((0, 0, 1, 0, 8), (1, 0, 1, 8, 8))
+NEAR = ((0, 4, 2, 0, 24), (1, 6, 2, 0, 24))
+FAR = ((0, 0, 2, 0, 24), (1, 2, 2, 0, 24))
+MIDDLE = ((0, 1, 1, 0, 24), (1, 2, 2, 0, 24))
+LAST = ((0, 0, 1, 0, 16), (1, 0, 1, 16, 8))
 PARTS = {(0, 0): NEAR, (0, 1): FAR, (1, 0): NEAR, (1, 1): MIDDLE, (1, 2): LAST}
 
 
@@ -35,7 +37,7 @@
 def kernel(
     tok, gw, uw, dw, cot,
     out, gt, gg, gu, gd,
-    acts, weights, rows_in, X, W, sent, got, part, final, H,
+    acts, weights, rows_in, X, W, WE, WP, sent, got, part, final, H,
     S, SR, T, RX, U, RY, acc, gsend, ggot, grads, rows_out, results,
     in_s, out_s, w_s, w_r, ag_s, ag_r, fw_s, fw_r, rs_s, rs_r, ga_s, ga_r, sx_s, sx_r, xy_s, xy_r, gr_s, gr_r,
 ):
@@ -69,6 +71,7 @@
     for device in [sibling, right, left, *xpeers.values(), *ypeers.values()]:
         pl.semaphore_signal(barrier, inc=1, device_id=device, device_id_type=MESH)
 
+    first_half = lax.broadcasted_iota(jnp.int32, (PIECE, LANES), 1) < TAIL
     loads = [
         pltpu.make_async_copy(src, dst, in_s.at[i])
         for i, (src, dst) in enumerate(
@@ -80,14 +83,21 @@
 
     def pieces(a):
         loads[a].wait()
-        rows_in[a] = dot(identity(HALF), acts[a], 1, 1).astype(BF16)
-        for o, d in enumerate(ORDER):
-            j = lax.rem(z + d, 8)
-            X[a, k, x, y, o] = rows_in[a, pl.ds(pl.multiple_of(j * PIECE, PIECE), PIECE), :]
+        one = identity(HALF)
+        tails = acts[a, pl.ds(LANES, TAIL), :]
+        rows_in[a, 0] = dot(one, acts[a, pl.ds(0, LANES), :], 1, 1)
+        rows_in[a, 1] = dot(one, jnp.concatenate([tails, tails], axis=0), 1, 1)
+        for q in range(4):
+            at = [pl.ds(pl.multiple_of(lax.rem(z + ORDER[2 * q + e], 8) * PIECE, PIECE), PIECE) for e in range(2)]
+            for e in range(2):
+                X[a, k, x, y, q, pl.ds(e * PIECE, PIECE), :] = rows_in[a, 0, at[e], :].astype(BF16)
+            X[a, k, x, y, q, pl.ds(2 * PIECE, PIECE), :] = jnp.where(
+                first_half, rows_in[a, 1, at[0], :], rows_in[a, 1, at[1], :]
+            ).astype(BF16)
 
     def gather1(a, c):
         for cls in range(2):
-            ref = X.at[a, k, x, y, pl.ds(4 * c + 2 * cls, 2)]
+            ref = X.at[a, k, x, y, 2 * c + cls]
             for i in (1, 2, 3):
                 start(
                     ("gather", a, c, cls, 0, i),
@@ -96,10 +106,10 @@
 
     def gather2(a, c):
         for cls in range(2):
-            places = pl.ds(4 * c + 2 * cls, 2)
+            q = 2 * c + cls
             for i in (1, 2, 3):
                 arrive("gather", a, c, cls, 0, i)
-            ref = X.at[a, k, :, y, places] if cls == 0 else X.at[a, k, x, :, places]
+            ref = X.at[a, k, :, y, q] if cls == 0 else X.at[a, k, x, :, q]
             for i in (1, 2, 3):
                 start(
                     ("gather", a, c, cls, 1, i),
@@ -110,7 +120,7 @@
         for cls in range(2):
             for i in (1, 2, 3):
                 arrive("gather", a, c, cls, 1, i)
-        ref = X.at[a, k, :, :, pl.ds(4 * c, 4)]
+        ref = X.at[a, k, :, :, pl.ds(2 * c, 2)]
         start(("pair", a, c), copy(ref, ref, fw_s.at[a, c], fw_r.at[a, c], sibling))
 
     def gather4(a, c):
@@ -125,12 +135,34 @@
             start(("weight", i), copy(weights.at[i, :, theirs], W.at[i, k], w_s.at[i], w_r.at[i], sibling))
         for i in range(3):
             W[i, k] = weights[i, :, mine]
+            expand(i, k)
+
+    def expand(i, h):
+        main, tail = W[i, h, pl.ds(0, LANES), :], W[i, h, pl.ds(LANES, TAIL), :]
+        none = jnp.zeros_like(tail)
+        for e in range(2):
+            WE[e, i, h, pl.ds(0, LANES), :] = main
+            WE[e, i, h, pl.ds(LANES + e * TAIL, TAIL), :] = tail
+            WE[e, i, h, pl.ds(LANES + (1 - e) * TAIL, TAIL), :] = none
+        WP[i, h, pl.ds(0, LANES), :] = main
+        for e in range(2):
+            WP[i, h, pl.ds(LANES + e * TAIL, TAIL), :] = tail
+
+    def expand_theirs():
+        for i in range(3):
+            arrive("weight", i)
+            expand(i, other)
+
+    def packed(a, h, q, e, first, rows):
+        span = pl.ds(first, rows // 64)
+        main = X[a, h, span, :, q, pl.ds(e * PIECE, PIECE), :].reshape(rows, LANES)
+        tail = X[a, h, span, :, q, pl.ds(2 * PIECE, PIECE), :].reshape(rows, LANES)
+        return jnp.concatenate([main, tail], axis=1)
 
     def local(a, o, first, rows):
         total = None
         for h in range(2):
-            block = X[a // 2, h, pl.ds(first, rows // 64), :, o].reshape(rows, width)
-            p = dot(block, W[a, h], 1, 0)
+            p = dot(packed(a // 2, h, o // 2, o % 2, first, rows), WE[o % 2, a, h], 1, 0)
             total = p if total is None else total + p
         return total
 
@@ -208,10 +240,13 @@
         def body(o, carry):
             for h in range(2):
                 if i == 0:
-                    p = dot(H[0, o], W[2, h], 1, 1)
+                    p = dot(H[0, o], WP[2, h], 1, 1)
                 else:
-                    p = dot(H[1, o], W[0, h], 1, 1) + dot(H[2, o], W[1, h], 1, 1)
-                S[i, h, :, :, o] = p.reshape(4, 4, PIECE, width)
+                    p = dot(H[1, o], WP[0, h], 1, 1) + dot(H[2, o], WP[1, h], 1, 1)
+                S[i, h, :, :, o, pl.ds(0, PIECE), :] = p[:, :LANES].reshape(4, 4, PIECE, LANES)
+                tail = p[:, LANES:].reshape(4, 4, PIECE, LANES)
+                low = lax.broadcasted_iota(jnp.int32, (4, 4, 8, LANES), 3) < TAIL
+                S[i, h, :, :, o, pl.ds(PIECE, 8), :] = jnp.where(low, tail[:, :, :8], tail[:, :, 8:])
             return carry
 
         if n == 1:
@@ -275,7 +310,7 @@
                 total = total + RY[i, q - 1, span, rows]
             for p in range(n):
                 j = lax.rem(z + ORDER[lo + p], 8)
-                rows_out[i, pl.ds(pl.multiple_of(j * PIECE + r, 8), m), :] = total[p]
+                rows_out[i, j, rows, :] = total[p]
 
     stores = []
 
@@ -285,15 +320,25 @@
         stores.append(c)
 
     def deliver(i):
-        results[i] = dot(identity(width), rows_out[i].astype(BF16), 1, 1).astype(BF16)
+        one = identity(LANES)
+        main = rows_out[i, :, pl.ds(0, PIECE), :].reshape(HALF, LANES)
+        tail = rows_out[i, :, pl.ds(PIECE, 8), :]
+        tail = jnp.concatenate([tail, tail], axis=1).reshape(HALF, LANES)
+        results[i, pl.ds(0, LANES), :] = dot(one, main.astype(BF16), 1, 1).astype(BF16)
+        tail = dot(one, tail.astype(BF16), 1, 1)
+        low = lax.broadcasted_iota(jnp.int32, (TAIL, HALF), 1) % PIECE < 8
+        results[i, pl.ds(LANES, TAIL), :] = jnp.where(low, tail[:TAIL], tail[TAIL:]).astype(BF16)
         store(results.at[i], (out, gt)[i])
 
     def grad(n, lo, hi):
         a, b = ((0, 1), (0, 2), (1, 0))[n]
 
-        def body(o, carry):
+        def body(q, carry):
             for h in range(2):
-                acc[n, h] += dot(X[a, h, :, :, o].reshape(BLOCK, width), H[b, o], 0, 0)
+                for e in range(2):
+                    p = dot(packed(a, h, q, e, 0, BLOCK), H[b, 2 * q + e], 0, 0)
+                    acc[n, h, pl.ds(0, LANES), :] += p[:LANES]
+                    acc[n, h, pl.ds(LANES, TAIL), :] += p[LANES + e * TAIL : LANES + (e + 1) * TAIL]
             return carry
 
         if hi - lo == 1:
@@ -315,40 +360,39 @@
     pl.semaphore_wait(barrier, 9)
     gather1(0, 0)
     swap_weights()
+    gather2(0, 0)
+    pieces(1)
+    gather1(1, 0)
     gather1(0, 1)
-    pieces(1)
-    gather2(0, 0)
-    gather1(1, 0)
     acc[...] = jnp.zeros_like(acc)
+    expand_theirs()
+    gather2(1, 0)
+    gather3(0, 0)
     gather2(0, 1)
-    gather3(0, 0)
-    gather2(1, 0)
     gather1(1, 1)
-    for i in range(3):
-        arrive("weight", i)
     gather4(0, 0)
     step0(0)
     step0(1)
-    gather3(0, 1)
+    gather3(1, 0)
+    gather2(1, 1)
     step(0, 1)
     step(1, 1)
-    gather3(1, 0)
-    gather2(1, 1)
+    gather3(0, 1)
+    gather4(1, 0)
+    step0(2)
     gather4(0, 1)
     step(0, 2)
     step(1, 2)
-    gather4(1, 0)
-    step0(2)
+    step(2, 1)
     gather3(1, 1)
     step(0, 3)
     step(1, 3)
-    step(2, 1)
     gather4(1, 1)
+    step(2, 2)
     finish(0)
     finish(1)
     activate()
     relay_step(0, 0)
-    step(2, 2)
     step(2, 3)
     relay_step(0, 1)
     finish(2)
@@ -359,29 +403,29 @@
     relay_step(1, 1)
     scatter1(0, 0)
     relay_step(0, 3)
-    grad(2, 4, 8)
+    grad(2, 2, 4)
     relay_step(1, 2)
     products(1, 0, 4, 4)
     relay_end(0)
     products(0, 1, 0, 4)
+    scatter2(0, 0)
     scatter1(1, 0)
-    grad(2, 0, 4)
+    scatter1(0, 1)
     relay_step(1, 3)
     products(1, 1, 1, 3)
-    scatter2(0, 0)
-    scatter1(0, 1)
+    grad(2, 0, 2)
+    grad_swap(2)
     scatter2(1, 0)
-    grad_swap(2)
     scatter1(1, 1)
-    grad(0, 1, 8)
-    grad(1, 1, 8)
+    scatter2(0, 1)
+    grad(0, 1, 4)
+    grad(1, 1, 4)
     relay_end(1)
     products(1, 2, 0, 1)
-    scatter2(0, 1)
+    scatter2(1, 1)
     grad(0, 0, 1)
     grad_swap(0)
     scatter1(1, 2)
-    scatter2(1, 1)
     grad(1, 0, 1)
     grad_swap(1)
     scatter3(0, 0)
@@ -402,12 +446,8 @@
 
 
 def hand_over(*refs):
-    sems = refs[10]
-    copies = [pltpu.make_async_copy(refs[i], refs[5 + i], sems.at[i]) for i in range(5)]
-    for c in copies:
-        c.start()
-    for c in copies:
-        c.wait()
+    for i in range(5):
+        refs[5 + i][...] = refs[i][...]
 
 
 def body(tokens, gate_weight, up_weight, down_weight, cotangent):
@@ -421,25 +461,27 @@
     scratch = [
         V((2, width, n_tok), BF16),
         V((3, width, hidden), BF16),
-        V((2, n_tok, width), BF16),
-        V((2, 2, 4, 4, 8, PIECE, width), BF16),
+        V((2, 2, n_tok, LANES), F32),
+        V((2, 2, 4, 4, 4, 3 * PIECE, LANES), BF16),
         V((3, 2, width, BLOCK), BF16),
+        V((2, 3, 2, 2 * LANES, BLOCK), BF16),
+        V((3, 2, 2 * LANES, BLOCK), BF16),
         V((3, 2, 4, BLOCK, BLOCK), BF16),
         V((3, 2, 4, BLOCK, BLOCK), BF16),
         V((2, BLOCK, BLOCK), F32),
         V((3, BLOCK, BLOCK), F32),
         V((3, 8, BLOCK, BLOCK), BF16),
-        V((2, 2, 4, 4, 8, PIECE, width), F32),
-        V((2, 4, 4, 8, PIECE, width), F32),
-        V((2, 4, 4, 8, PIECE, width), F32),
-        V((2, 3, 4, 8, PIECE, width), F32),
-        V((2, 4, 8, PIECE, width), F32),
-        V((2, 3, 8, PIECE, width), F32),
+        V((2, 2, 4, 4, 8, 24, LANES), F32),
+        V((2, 4, 4, 8, 24, LANES), F32),
+        V((2, 4, 4, 8, 24, LANES), F32),
+        V((2, 3, 4, 8, 24, LANES), F32),
+        V((2, 4, 8, 24, LANES), F32),
+        V((2, 3, 8, 24, LANES), F32),
         V((3, 2, width, BLOCK), F32),
         V((3, width, BLOCK), BF16),
         V((3, width, BLOCK), BF16),
         V((3, width, hidden), BF16),
-        V((2, n_tok, width), F32),
+        V((2, 8, 24, LANES), F32),
         V((2, width, n_tok), BF16),
         dma((5,)), dma((5,)),
         dma((3,)), dma((3,)),
@@ -463,14 +505,13 @@
             collective_id=0, has_side_effects=True, vmem_limit_bytes=56 * 2**20
         ),
     )(tokens.T, gate_weight, up_weight, down_weight.T, cotangent.T)
+    vmem = pl.BlockSpec(memory_space=pltpu.VMEM)
     results = pl.pallas_call(
         hand_over,
         out_shape=shapes,
-        in_specs=[anywhere] * 5,
-        out_specs=(anywhere,) * 5,
-        scratch_shapes=[dma((5,))],
+        in_specs=[vmem] * 5,
+        out_specs=(vmem,) * 5,
         name="hand_over",
-        compiler_params=pltpu.CompilerParams(vmem_limit_bytes=60 * 2**20),
     )(*held)
     return results[0].T, results[1].T, results[2], results[3], results[4].T
 

time: 136 us -> 108 us (0.79)
  Pallas kernels: 135 us -> 107 us
    pallas_call x1, Pallas kernels: 22 us -> 2.01 us  [body(): pl.pallas_call(hand_over, out_shape=shapes, in_specs=[vmem] * 5, out_spec...]
    pallas_call x1, Pallas kernels: 113 us -> 105 us  [body(): pl.pallas_call(kernel, out_shape=shapes, in_specs=[anywhere] * 5, out_spe...]
where the time goes in v3:
time: 108 us
  Pallas kernels  107 us (99%)
    pallas_call x1, Pallas kernels, body(): pl.pallas_call(kernel, out_shape=shapes, in_specs=[anywhere] * 5, out_spe...  105 us

profile of v3, /device:TPU:1, one launch (start us, length us, event | category | flops | bytes accessed | tf_op | source)
XLA Modules:
  0.0 107.8 jit_solution(994343867342088767)
XLA Ops:
  0.6 105.2 %feed_forward.1 = (bf16[192,128]{1,0:T(8,128)(2,1)}, bf16[192,128]{1,0:T(8,128)(2,1)}, bf16[192,512]{1,0:T(8,128)(2,1)}, bf16[192,512]{1,0:T(8,128)(2,1)}, bf16[192,512]{1,0:T(8,128)(2,1)}) custom-call(bf16[192,128]{1,0:T(8,128)(2,1)} %bitcast.7, bf16[192,512]{1,0:T(8,128)(2,1)} %gw.1, bf16[192,512]{1,0:T(8,128)(2,1)} %uw.1, bf16[192,512]{1,0:T(8,128)(2,1)} %bitcast.6, ...), custom_call_target="tpu_custom_call" | custom-call | tf_op jit(solution)/shard_map/feed_forward/pallas_call | solution.py:497
  105.8 2.0 %hand_over.1 = (bf16[192,128]{1,0:T(8,128)(2,1)}, bf16[192,128]{1,0:T(8,128)(2,1)}, bf16[192,512]{1,0:T(8,128)(2,1)}, bf16[192,512]{1,0:T(8,128)(2,1)}, bf16[192,512]{1,0:T(8,128)(2,1)}) custom-call(bf16[192,128]{1,0:T(8,128)(2,1)} %get-tuple-element.15.refs_0_, bf16[192,128]{1,0:T(8,128)(2,1)} %get-tuple-element.16.refs_1_, ...), custom_call_target="tpu_custom_call" | custom-call | tf_op jit(solution)/shard_map/hand_over/pallas_call | solution.py:509

commit v4 on v3

--- a/solution.py
+++ b/solution.py
@@ -18,11 +18,20 @@
 HALF = 128
 RIGHTWARD = tuple(PLACE[d] for d in (0, 7, 6, 5, 4))
 LEFTWARD = tuple(PLACE[d] for d in (0, 1, 2, 3, 4))
-NEAR = ((0, 4, 2, 0, 24), (1, 6, 2, 0, 24))
-FAR = ((0, 0, 2, 0, 24), (1, 2, 2, 0, 24))
-MIDDLE = ((0, 1, 1, 0, 24), (1, 2, 2, 0, 24))
-LAST = ((0, 0, 1, 0, 16), (1, 0, 1, 16, 8))
-PARTS = {(0, 0): NEAR, (0, 1): FAR, (1, 0): NEAR, (1, 1): MIDDLE, (1, 2): LAST}
+PARTS = (
+    (
+        (0, 4, 2, 0, 24), (1, 6, 2, 0, 24),
+        (0, 1, 1, 0, 24), (1, 2, 1, 0, 24), (0, 3, 1, 0, 16), (1, 3, 1, 16, 8),
+        (0, 0, 1, 0, 8), (1, 0, 1, 8, 16),
+    ),
+    (
+        (0, 5, 1, 0, 24), (1, 7, 1, 0, 24), (0, 3, 1, 0, 8), (1, 3, 1, 8, 16),
+        (0, 4, 1, 0, 24), (1, 6, 1, 0, 24),
+        (0, 1, 1, 0, 24), (1, 2, 1, 0, 24),
+        (0, 0, 1, 0, 16), (1, 0, 1, 16, 8),
+    ),
+)
+GROUPS = (((0, 1), (2, 3, 4, 5), (6, 7)), ((0, 1, 2, 3), (4, 5), (6, 7), (8, 9)))
 
 
 def dot(a, b, ca, cb):
@@ -67,6 +76,14 @@
     def arrive(*key):
         started[key].wait_recv()
 
+    sent_off = []
+
+    def settle(but=0):
+        for key in list(started)[: len(started) - but]:
+            if key not in sent_off:
+                started[key].wait_send()
+                sent_off.append(key)
+
     barrier = pltpu.get_barrier_semaphore()
     for device in [sibling, right, left, *xpeers.values(), *ypeers.values()]:
         pl.semaphore_signal(barrier, inc=1, device_id=device, device_id_type=MESH)
@@ -205,7 +222,6 @@
         final[a] += got[a, 0, 3].astype(F32) + got[a, 1, 3].astype(F32)
 
     def relay_step(m, s):
-        lo, n = (0, 1) if m == 0 else (1, 2)
         for dr in range(2):
             places = (RIGHTWARD, LEFTWARD)[dr]
             rows = half(dr) if s == 3 else pl.ds(0, BLOCK)
@@ -214,8 +230,8 @@
             start(
                 ("relay", m, dr, s),
                 copy(
-                    H.at[pl.ds(lo, n), places[s], rows],
-                    H.at[pl.ds(lo, n), places[s + 1], rows],
+                    H.at[m, places[s], rows],
+                    H.at[m, places[s + 1], rows],
                     ga_s.at[m, dr, s],
                     ga_r.at[m, dr, s],
                     (right, left)[dr],
@@ -236,7 +252,7 @@
         H[1, PLACE[0]] = (gh * up * sigma * (1.0 + gate * (1.0 - sigma))).astype(BF16)
         H[2, PLACE[0]] = (gh * (gate * sigma)).astype(BF16)
 
-    def products(i, g, lo, n):
+    def product(i, lo, n):
         def body(o, carry):
             for h in range(2):
                 if i == 0:
@@ -253,16 +269,32 @@
             body(lo, 0)
         else:
             lax.fori_loop(lo, lo + n, body, 0)
-        span = pl.ds(lo, n)
-        start(
-            ("cores", i, g),
-            copy(S.at[i, other, :, :, span], SR.at[i, :, :, span], sx_s.at[i, g], sx_r.at[i, g], sibling),
-        )
+
+    def part_of(i, u):
+        cls, lo, n, r, m = PARTS[i][u]
+        return cls, lo, n, pl.ds(lo, n), pl.ds(r, m)
+
+    def products(i, g):
+        for lo, n in dict.fromkeys(PARTS[i][u][1:3] for u in GROUPS[i][g]):
+            product(i, lo, n)
+            for u in GROUPS[i][g]:
+                if PARTS[i][u][1] == lo:
+                    cls, lo, n, span, rows = part_of(i, u)
+                    start(
+                        ("cores", i, u),
+                        copy(
+                            S.at[i, other, :, :, span, rows],
+                            SR.at[i, :, :, span, rows],
+                            sx_s.at[i, u],
+                            sx_r.at[i, u],
+                            sibling,
+                        ),
+                    )
 
     def scatter1(i, g):
-        arrive("cores", i, g)
-        for cls, lo, n, r, m in PARTS[i, g]:
-            span, rows = pl.ds(lo, n), pl.ds(r, m)
+        for u in GROUPS[i][g]:
+            cls, lo, n, span, rows = part_of(i, u)
+            arrive("cores", i, u)
             T[i, :, :, span, rows] = S[i, k, :, :, span, rows] + SR[i, :, :, span, rows]
             for q in (1, 2, 3):
                 if cls == 0:
@@ -270,47 +302,46 @@
                 else:
                     src = T.at[i, :, lax.rem(y + q, 4), span, rows]
                 start(
-                    ("scatter", i, g, cls, 0, q),
+                    ("scatter", i, u, 0, q),
                     copy(
                         src,
                         RX.at[i, q - 1, :, span, rows],
-                        xy_s.at[i, g, cls, 0, q - 1],
-                        xy_r.at[i, g, cls, 0, q - 1],
+                        xy_s.at[i, u, 0, q - 1],
+                        xy_r.at[i, u, 0, q - 1],
                         peers[cls][q],
                     ),
                 )
 
     def scatter2(i, g):
-        for cls, lo, n, r, m in PARTS[i, g]:
-            span, rows = pl.ds(lo, n), pl.ds(r, m)
+        for u in GROUPS[i][g]:
+            cls, lo, n, span, rows = part_of(i, u)
             total = T[i, x, :, span, rows] if cls == 0 else T[i, :, y, span, rows]
             for q in (1, 2, 3):
-                arrive("scatter", i, g, cls, 0, q)
+                arrive("scatter", i, u, 0, q)
                 total = total + RX[i, q - 1, :, span, rows]
             U[i, :, span, rows] = total
             for q in (1, 2, 3):
                 at = lax.rem(y + q, 4) if cls == 0 else lax.rem(x + q, 4)
                 start(
-                    ("scatter", i, g, cls, 1, q),
+                    ("scatter", i, u, 1, q),
                     copy(
                         U.at[i, at, span, rows],
                         RY.at[i, q - 1, span, rows],
-                        xy_s.at[i, g, cls, 1, q - 1],
-                        xy_r.at[i, g, cls, 1, q - 1],
+                        xy_s.at[i, u, 1, q - 1],
+                        xy_r.at[i, u, 1, q - 1],
                         peers[1 - cls][q],
                     ),
                 )
 
     def scatter3(i, g):
-        for cls, lo, n, r, m in PARTS[i, g]:
-            span, rows = pl.ds(lo, n), pl.ds(r, m)
+        for u in GROUPS[i][g]:
+            cls, lo, n, span, rows = part_of(i, u)
             total = U[i, y if cls == 0 else x, span, rows]
             for q in (1, 2, 3):
-                arrive("scatter", i, g, cls, 1, q)
+                arrive("scatter", i, u, 1, q)
                 total = total + RY[i, q - 1, span, rows]
             for p in range(n):
-                j = lax.rem(z + ORDER[lo + p], 8)
-                rows_out[i, j, rows, :] = total[p]
+                rows_out[i, lax.rem(z + ORDER[lo + p], 8), rows, :] = total[p]
 
     stores = []
 
@@ -398,56 +429,78 @@
     finish(2)
     activate_back()
     relay_step(1, 0)
+    relay_step(2, 0)
     relay_step(0, 2)
-    products(0, 0, 4, 4)
+    products(0, 0)
     relay_step(1, 1)
     scatter1(0, 0)
+    relay_step(2, 1)
+    products(1, 0)
+    grad(2, 2, 4)
     relay_step(0, 3)
-    grad(2, 2, 4)
+    products(0, 1)
+    scatter1(1, 0)
+    scatter2(0, 0)
     relay_step(1, 2)
-    products(1, 0, 4, 4)
+    scatter1(0, 1)
+    relay_step(2, 2)
+    products(1, 1)
+    scatter2(1, 0)
     relay_end(0)
-    products(0, 1, 0, 4)
-    scatter2(0, 0)
-    scatter1(1, 0)
-    scatter1(0, 1)
-    relay_step(1, 3)
-    products(1, 1, 1, 3)
+    products(0, 2)
+    scatter1(1, 1)
     grad(2, 0, 2)
     grad_swap(2)
-    scatter2(1, 0)
-    scatter1(1, 1)
+    scatter1(0, 2)
+    relay_step(1, 3)
     scatter2(0, 1)
+    relay_step(2, 3)
+    settle(24)
+    products(1, 2)
+    scatter2(1, 1)
+    scatter2(0, 2)
     grad(0, 1, 4)
+    scatter1(1, 2)
     grad(1, 1, 4)
     relay_end(1)
-    products(1, 2, 0, 1)
-    scatter2(1, 1)
+    relay_end(2)
+    products(1, 3)
     grad(0, 0, 1)
     grad_swap(0)
-    scatter1(1, 2)
+    scatter1(1, 3)
     grad(1, 0, 1)
     grad_swap(1)
+    scatter2(1, 2)
     scatter3(0, 0)
     scatter3(0, 1)
+    scatter3(0, 2)
     deliver(0)
+    scatter2(1, 3)
     grad_end(2)
-    scatter2(1, 2)
     scatter3(1, 0)
+    scatter3(1, 1)
     grad_end(0)
     grad_end(1)
-    scatter3(1, 1)
+    settle(8)
     scatter3(1, 2)
+    scatter3(1, 3)
     deliver(1)
     for c in stores:
         c.wait()
-    for c in started.values():
-        c.wait_send()
+    settle()
 
 
 def hand_over(*refs):
-    for i in range(5):
-        refs[5 + i][...] = refs[i][...]
+    held, results, kept, sems = refs[:5], refs[5:10], refs[10:15], refs[15]
+    loads = [pltpu.make_async_copy(held[i], kept[i], sems.at[0, i]) for i in range(5)]
+    stores = [pltpu.make_async_copy(kept[i], results[i], sems.at[1, i]) for i in range(5)]
+    for c in loads:
+        c.start()
+    for load, store in zip(loads, stores):
+        load.wait()
+        store.start()
+    for c in stores:
+        c.wait()
 
 
 def body(tokens, gate_weight, up_weight, down_weight, cotangent):
@@ -488,9 +541,9 @@
         dma((2, 2, 2, 2, 3)), dma((2, 2, 2, 2, 3)),
         dma((2, 2)), dma((2, 2)),
         dma((3, 2, 4)), dma((3, 2, 4)),
-        dma((2, 2, 4)), dma((2, 2, 4)),
-        dma((2, 3)), dma((2, 3)),
-        dma((2, 3, 2, 2, 3)), dma((2, 3, 2, 2, 3)),
+        dma((3, 2, 4)), dma((3, 2, 4)),
+        dma((2, 10)), dma((2, 10)),
+        dma((2, 10, 2, 3)), dma((2, 10, 2, 3)),
         dma((3,)), dma((3,)),
     ]
     anywhere = pl.BlockSpec(memory_space=pl.ANY)
@@ -505,13 +558,14 @@
             collective_id=0, has_side_effects=True, vmem_limit_bytes=56 * 2**20
         ),
     )(tokens.T, gate_weight, up_weight, down_weight.T, cotangent.T)
-    vmem = pl.BlockSpec(memory_space=pltpu.VMEM)
     results = pl.pallas_call(
         hand_over,
         out_shape=shapes,
-        in_specs=[vmem] * 5,
-        out_specs=(vmem,) * 5,
+        in_specs=[anywhere] * 5,
+        out_specs=(anywhere,) * 5,
+        scratch_shapes=[V(v.shape, BF16) for v in shapes] + [dma((2, 5))],
         name="hand_over",
+        compiler_params=pltpu.CompilerParams(vmem_limit_bytes=60 * 2**20),
     )(*held)
     return results[0].T, results[1].T, results[2], results[3], results[4].T
 

time: 108 us -> 101 us (0.935)
  Pallas kernels: 107 us -> 101 us
    pallas_call x1, Pallas kernels: 105 us -> 98.6 us  [body(): pl.pallas_call(kernel, out_shape=shapes, in_specs=[anywhere] * 5, out_spe...]
where the time goes in v4:
time: 101 us
  Pallas kernels  101 us (100%)
    pallas_call x1, Pallas kernels, body(): pl.pallas_call(kernel, out_shape=shapes, in_specs=[anywhere] * 5, out_spe...  98.6 us

profile of v4, /device:TPU:1, one launch (start us, length us, event | category | flops | bytes accessed | tf_op | source)
XLA Modules:
  0.0 101.2 jit_solution(10234985582035452082)
XLA Ops:
  0.6 98.6 %feed_forward.1 = (bf16[192,128]{1,0:T(8,128)(2,1)}, bf16[192,128]{1,0:T(8,128)(2,1)}, bf16[192,512]{1,0:T(8,128)(2,1)}, bf16[192,512]{1,0:T(8,128)(2,1)}, bf16[192,512]{1,0:T(8,128)(2,1)}) custom-call(bf16[192,128]{1,0:T(8,128)(2,1)} %bitcast.7, bf16[192,512]{1,0:T(8,128)(2,1)} %gw.1, bf16[192,512]{1,0:T(8,128)(2,1)} %uw.1, bf16[192,512]{1,0:T(8,128)(2,1)} %bitcast.6, ...), custom_call_target="tpu_custom_call" | custom-call | tf_op jit(solution)/shard_map/feed_forward/pallas_call | solution.py:550
  99.2 1.9 %hand_over.1 = (bf16[192,128]{1,0:T(8,128)(2,1)}, bf16[192,128]{1,0:T(8,128)(2,1)}, bf16[192,512]{1,0:T(8,128)(2,1)}, bf16[192,512]{1,0:T(8,128)(2,1)}, bf16[192,512]{1,0:T(8,128)(2,1)}) custom-call(bf16[192,128]{1,0:T(8,128)(2,1)} %get-tuple-element.15.refs_0_, bf16[192,128]{1,0:T(8,128)(2,1)} %get-tuple-element.16.refs_1_, ...), custom_call_target="tpu_custom_call" | custom-call | tf_op jit(solution)/shard_map/hand_over/pallas_call | solution.py:561

commit v5 on v4

--- a/solution.py
+++ b/solution.py
@@ -137,11 +137,11 @@
         for cls in range(2):
             for i in (1, 2, 3):
                 arrive("gather", a, c, cls, 1, i)
-        ref = X.at[a, k, :, :, pl.ds(2 * c, 2)]
-        start(("pair", a, c), copy(ref, ref, fw_s.at[a, c], fw_r.at[a, c], sibling))
-
-    def gather4(a, c):
-        arrive("pair", a, c)
+            ref = X.at[a, k, :, :, 2 * c + cls]
+            start(("pair", a, c, cls), copy(ref, ref, fw_s.at[a, c, cls], fw_r.at[a, c, cls], sibling))
+
+    def gather4(a, c, cls):
+        arrive("pair", a, c, cls)
 
     mine = pl.ds(pl.multiple_of(k * BLOCK, BLOCK), BLOCK)
     theirs = pl.ds(pl.multiple_of(other * BLOCK, BLOCK), BLOCK)
@@ -397,28 +397,32 @@
     gather1(0, 1)
     acc[...] = jnp.zeros_like(acc)
     expand_theirs()
+    gather3(0, 0)
     gather2(1, 0)
-    gather3(0, 0)
     gather2(0, 1)
     gather1(1, 1)
-    gather4(0, 0)
+    gather4(0, 0, 0)
     step0(0)
     step0(1)
+    gather4(0, 0, 1)
     gather3(1, 0)
     gather2(1, 1)
     step(0, 1)
     step(1, 1)
     gather3(0, 1)
-    gather4(1, 0)
+    gather4(1, 0, 0)
     step0(2)
-    gather4(0, 1)
+    gather4(0, 1, 0)
+    gather4(0, 1, 1)
     step(0, 2)
     step(1, 2)
+    gather4(1, 0, 1)
     step(2, 1)
     gather3(1, 1)
     step(0, 3)
     step(1, 3)
-    gather4(1, 1)
+    gather4(1, 1, 0)
+    gather4(1, 1, 1)
     step(2, 2)
     finish(0)
     finish(1)
@@ -459,23 +463,21 @@
     products(1, 2)
     scatter2(1, 1)
     scatter2(0, 2)
-    grad(0, 1, 4)
     scatter1(1, 2)
-    grad(1, 1, 4)
     relay_end(1)
     relay_end(2)
     products(1, 3)
-    grad(0, 0, 1)
+    grad(0, 0, 4)
     grad_swap(0)
     scatter1(1, 3)
-    grad(1, 0, 1)
+    scatter2(1, 2)
+    grad(1, 0, 4)
     grad_swap(1)
-    scatter2(1, 2)
     scatter3(0, 0)
     scatter3(0, 1)
     scatter3(0, 2)
+    scatter2(1, 3)
     deliver(0)
-    scatter2(1, 3)
     grad_end(2)
     scatter3(1, 0)
     scatter3(1, 1)
@@ -539,7 +541,7 @@
         dma((5,)), dma((5,)),
         dma((3,)), dma((3,)),
         dma((2, 2, 2, 2, 3)), dma((2, 2, 2, 2, 3)),
-        dma((2, 2)), dma((2, 2)),
+        dma((2, 2, 2)), dma((2, 2, 2)),
         dma((3, 2, 4)), dma((3, 2, 4)),
         dma((3, 2, 4)), dma((3, 2, 4)),
         dma((2, 10)), dma((2, 10)),

time: 101 us -> 100 us (0.990)
  Pallas kernels: 101 us -> 99 us
    pallas_call x1, Pallas kernels: 98.6 us -> 97.1 us  [body(): pl.pallas_call(kernel, out_shape=shapes, in_specs=[anywhere] * 5, out_spe...]
where the time goes in v5:
time: 100 us; the launch traced here: 99.6 us
  Pallas kernels  99 us (99%)
    pallas_call x1, Pallas kernels, body(): pl.pallas_call(kernel, out_shape=shapes, in_specs=[anywhere] * 5, out_spe...  97.1 us

profile of v5, /device:TPU:1, one launch (start us, length us, event | category | flops | bytes accessed | tf_op | source)
XLA Modules:
  0.0 99.6 jit_solution(5840220543312943966)
XLA Ops:
  0.6 97.1 %feed_forward.1 = (bf16[192,128]{1,0:T(8,128)(2,1)}, bf16[192,128]{1,0:T(8,128)(2,1)}, bf16[192,512]{1,0:T(8,128)(2,1)}, bf16[192,512]{1,0:T(8,128)(2,1)}, bf16[192,512]{1,0:T(8,128)(2,1)}) custom-call(bf16[192,128]{1,0:T(8,128)(2,1)} %bitcast.7, bf16[192,512]{1,0:T(8,128)(2,1)} %gw.1, bf16[192,512]{1,0:T(8,128)(2,1)} %uw.1, bf16[192,512]{1,0:T(8,128)(2,1)} %bitcast.6, ...), custom_call_target="tpu_custom_call" | custom-call | tf_op jit(solution)/shard_map/feed_forward/pallas_call | solution.py:552
  97.7 1.9 %hand_over.1 = (bf16[192,128]{1,0:T(8,128)(2,1)}, bf16[192,128]{1,0:T(8,128)(2,1)}, bf16[192,512]{1,0:T(8,128)(2,1)}, bf16[192,512]{1,0:T(8,128)(2,1)}, bf16[192,512]{1,0:T(8,128)(2,1)}) custom-call(bf16[192,128]{1,0:T(8,128)(2,1)} %get-tuple-element.15.refs_0_, bf16[192,128]{1,0:T(8,128)(2,1)} %get-tuple-element.16.refs_1_, ...), custom_call_target="tpu_custom_call" | custom-call | tf_op jit(solution)/shard_map/hand_over/pallas_call | solution.py:563

commit v6 on v5

--- a/solution.py
+++ b/solution.py
@@ -28,10 +28,10 @@
         (0, 5, 1, 0, 24), (1, 7, 1, 0, 24), (0, 3, 1, 0, 8), (1, 3, 1, 8, 16),
         (0, 4, 1, 0, 24), (1, 6, 1, 0, 24),
         (0, 1, 1, 0, 24), (1, 2, 1, 0, 24),
-        (0, 0, 1, 0, 16), (1, 0, 1, 16, 8),
+        (0, 0, 1, 0, 24),
     ),
 )
-GROUPS = (((0, 1), (2, 3, 4, 5), (6, 7)), ((0, 1, 2, 3), (4, 5), (6, 7), (8, 9)))
+GROUPS = (((0, 1), (2, 3, 4, 5), (6, 7)), ((0, 1, 2, 3), (4, 5), (6, 7), (8,)))
 
 
 def dot(a, b, ca, cb):
@@ -47,8 +47,8 @@
     tok, gw, uw, dw, cot,
     out, gt, gg, gu, gd,
     acts, weights, rows_in, X, W, WE, WP, sent, got, part, final, H,
-    S, SR, T, RX, U, RY, acc, gsend, ggot, grads, rows_out, results,
-    in_s, out_s, w_s, w_r, ag_s, ag_r, fw_s, fw_r, rs_s, rs_r, ga_s, ga_r, sx_s, sx_r, xy_s, xy_r, gr_s, gr_r,
+    S, SR, T, RX, U, RY, RD, acc, gsend, ggot, grads, rows_out, results,
+    in_s, out_s, w_s, w_r, di_s, di_r, ag_s, ag_r, fw_s, fw_r, rs_s, rs_r, ga_s, ga_r, sx_s, sx_r, xy_s, xy_r, gr_s, gr_r, ld_s, ld_r,
 ):
     row, col = lax.axis_index("row"), lax.axis_index("col")
     z, k = row // 2, row % 2
@@ -61,6 +61,7 @@
     xpeers = {i: (row, lax.rem(x + i, 4) * 4 + y) for i in (1, 2, 3)}
     ypeers = {i: (row, x * 4 + lax.rem(y + i, 4)) for i in (1, 2, 3)}
     peers = (xpeers, ypeers)
+    plane = [(row, lax.rem(x + i, 4) * 4 + lax.rem(y + j, 4)) for i in range(4) for j in range(4)][1:]
 
     def copy(src, dst, s, r, device):
         return pltpu.make_async_remote_copy(
@@ -85,7 +86,7 @@
                 sent_off.append(key)
 
     barrier = pltpu.get_barrier_semaphore()
-    for device in [sibling, right, left, *xpeers.values(), *ypeers.values()]:
+    for device in [sibling, right, left, *plane]:
         pl.semaphore_signal(barrier, inc=1, device_id=device, device_id_type=MESH)
 
     first_half = lax.broadcasted_iota(jnp.int32, (PIECE, LANES), 1) < TAIL
@@ -107,41 +108,50 @@
         for q in range(4):
             at = [pl.ds(pl.multiple_of(lax.rem(z + ORDER[2 * q + e], 8) * PIECE, PIECE), PIECE) for e in range(2)]
             for e in range(2):
-                X[a, k, x, y, q, pl.ds(e * PIECE, PIECE), :] = rows_in[a, 0, at[e], :].astype(BF16)
-            X[a, k, x, y, q, pl.ds(2 * PIECE, PIECE), :] = jnp.where(
+                X[a, k, q, x, y, pl.ds(e * PIECE, PIECE), :] = rows_in[a, 0, at[e], :].astype(BF16)
+            X[a, k, q, x, y, pl.ds(2 * PIECE, PIECE), :] = jnp.where(
                 first_half, rows_in[a, 1, at[0], :], rows_in[a, 1, at[1], :]
             ).astype(BF16)
 
-    def gather1(a, c):
-        for cls in range(2):
-            ref = X.at[a, k, x, y, 2 * c + cls]
-            for i in (1, 2, 3):
-                start(
-                    ("gather", a, c, cls, 0, i),
-                    copy(ref, ref, ag_s.at[a, c, cls, 0, i - 1], ag_r.at[a, c, cls, 0, i - 1], peers[cls][i]),
-                )
-
-    def gather2(a, c):
-        for cls in range(2):
-            q = 2 * c + cls
-            for i in (1, 2, 3):
-                arrive("gather", a, c, cls, 0, i)
-            ref = X.at[a, k, :, y, q] if cls == 0 else X.at[a, k, x, :, q]
-            for i in (1, 2, 3):
-                start(
-                    ("gather", a, c, cls, 1, i),
-                    copy(ref, ref, ag_s.at[a, c, cls, 1, i - 1], ag_r.at[a, c, cls, 1, i - 1], peers[1 - cls][i]),
-                )
-
-    def gather3(a, c):
-        for cls in range(2):
-            for i in (1, 2, 3):
-                arrive("gather", a, c, cls, 1, i)
-            ref = X.at[a, k, :, :, 2 * c + cls]
-            start(("pair", a, c, cls), copy(ref, ref, fw_s.at[a, c, cls], fw_r.at[a, c, cls], sibling))
-
-    def gather4(a, c, cls):
-        arrive("pair", a, c, cls)
+    def direct1(a, q):
+        ref = X.at[a, k, q, x, y]
+        for i, device in enumerate(plane):
+            start(("direct", a, q, i), copy(ref, ref, di_s.at[i], di_r.at[i], device))
+
+    def direct2(a, q):
+        for i in range(15):
+            arrive("direct", a, q, i)
+        to_sibling(a, q)
+
+    def gather1(a, q):
+        ref = X.at[a, k, q, x, y]
+        for i in (1, 2, 3):
+            start(
+                ("gather", a, q, 0, i),
+                copy(ref, ref, ag_s.at[a, q, 0, i - 1], ag_r.at[a, q, 0, i - 1], peers[q % 2][i]),
+            )
+
+    def gather2(a, q):
+        for i in (1, 2, 3):
+            arrive("gather", a, q, 0, i)
+        ref = X.at[a, k, q, :, y] if q % 2 == 0 else X.at[a, k, q, x, :]
+        for i in (1, 2, 3):
+            start(
+                ("gather", a, q, 1, i),
+                copy(ref, ref, ag_s.at[a, q, 1, i - 1], ag_r.at[a, q, 1, i - 1], peers[1 - q % 2][i]),
+            )
+
+    def gather3(a, q):
+        for i in (1, 2, 3):
+            arrive("gather", a, q, 1, i)
+        to_sibling(a, q)
+
+    def to_sibling(a, q):
+        ref = X.at[a, k, q]
+        start(("pair", a, q), copy(ref, ref, fw_s.at[a, q], fw_r.at[a, q], sibling))
+
+    def gather4(a, q):
+        arrive("pair", a, q)
 
     mine = pl.ds(pl.multiple_of(k * BLOCK, BLOCK), BLOCK)
     theirs = pl.ds(pl.multiple_of(other * BLOCK, BLOCK), BLOCK)
@@ -172,8 +182,8 @@
 
     def packed(a, h, q, e, first, rows):
         span = pl.ds(first, rows // 64)
-        main = X[a, h, span, :, q, pl.ds(e * PIECE, PIECE), :].reshape(rows, LANES)
-        tail = X[a, h, span, :, q, pl.ds(2 * PIECE, PIECE), :].reshape(rows, LANES)
+        main = X[a, h, q, span, :, pl.ds(e * PIECE, PIECE), :].reshape(rows, LANES)
+        tail = X[a, h, q, span, :, pl.ds(2 * PIECE, PIECE), :].reshape(rows, LANES)
         return jnp.concatenate([main, tail], axis=1)
 
     def local(a, o, first, rows):
@@ -259,10 +269,10 @@
                     p = dot(H[0, o], WP[2, h], 1, 1)
                 else:
                     p = dot(H[1, o], WP[0, h], 1, 1) + dot(H[2, o], WP[1, h], 1, 1)
-                S[i, h, :, :, o, pl.ds(0, PIECE), :] = p[:, :LANES].reshape(4, 4, PIECE, LANES)
+                S[i, h, o, :, :, pl.ds(0, PIECE), :] = p[:, :LANES].reshape(4, 4, PIECE, LANES)
                 tail = p[:, LANES:].reshape(4, 4, PIECE, LANES)
                 low = lax.broadcasted_iota(jnp.int32, (4, 4, 8, LANES), 3) < TAIL
-                S[i, h, :, :, o, pl.ds(PIECE, 8), :] = jnp.where(low, tail[:, :, :8], tail[:, :, 8:])
+                S[i, h, o, :, :, pl.ds(PIECE, 8), :] = jnp.where(low, tail[:, :, :8], tail[:, :, 8:])
             return carry
 
         if n == 1:
@@ -283,8 +293,8 @@
                     start(
                         ("cores", i, u),
                         copy(
-                            S.at[i, other, :, :, span, rows],
-                            SR.at[i, :, :, span, rows],
+                            S.at[i, other, span, :, :, rows],
+                            SR.at[i, span, :, :, rows],
                             sx_s.at[i, u],
                             sx_r.at[i, u],
                             sibling,
@@ -295,17 +305,17 @@
         for u in GROUPS[i][g]:
             cls, lo, n, span, rows = part_of(i, u)
             arrive("cores", i, u)
-            T[i, :, :, span, rows] = S[i, k, :, :, span, rows] + SR[i, :, :, span, rows]
+            T[i, span, :, :, rows] = S[i, k, span, :, :, rows] + SR[i, span, :, :, rows]
             for q in (1, 2, 3):
                 if cls == 0:
-                    src = T.at[i, lax.rem(x + q, 4), :, span, rows]
+                    src = T.at[i, span, lax.rem(x + q, 4), :, rows]
                 else:
-                    src = T.at[i, :, lax.rem(y + q, 4), span, rows]
+                    src = T.at[i, span, :, lax.rem(y + q, 4), rows]
                 start(
                     ("scatter", i, u, 0, q),
                     copy(
                         src,
-                        RX.at[i, q - 1, :, span, rows],
+                        RX.at[i, q - 1, span, :, rows],
                         xy_s.at[i, u, 0, q - 1],
                         xy_r.at[i, u, 0, q - 1],
                         peers[cls][q],
@@ -315,17 +325,17 @@
     def scatter2(i, g):
         for u in GROUPS[i][g]:
             cls, lo, n, span, rows = part_of(i, u)
-            total = T[i, x, :, span, rows] if cls == 0 else T[i, :, y, span, rows]
+            total = T[i, span, x, :, rows] if cls == 0 else T[i, span, :, y, rows]
             for q in (1, 2, 3):
                 arrive("scatter", i, u, 0, q)
-                total = total + RX[i, q - 1, :, span, rows]
-            U[i, :, span, rows] = total
+                total = total + RX[i, q - 1, span, :, rows]
+            U[i, span, :, rows] = total
             for q in (1, 2, 3):
                 at = lax.rem(y + q, 4) if cls == 0 else lax.rem(x + q, 4)
                 start(
                     ("scatter", i, u, 1, q),
                     copy(
-                        U.at[i, at, span, rows],
+                        U.at[i, span, at, rows],
                         RY.at[i, q - 1, span, rows],
                         xy_s.at[i, u, 1, q - 1],
                         xy_r.at[i, u, 1, q - 1],
@@ -336,12 +346,28 @@
     def scatter3(i, g):
         for u in GROUPS[i][g]:
             cls, lo, n, span, rows = part_of(i, u)
-            total = U[i, y if cls == 0 else x, span, rows]
+            total = U[i, span, y if cls == 0 else x, rows]
             for q in (1, 2, 3):
                 arrive("scatter", i, u, 1, q)
                 total = total + RY[i, q - 1, span, rows]
             for p in range(n):
                 rows_out[i, lax.rem(z + ORDER[lo + p], 8), rows, :] = total[p]
+
+    def last1(i, u):
+        arrive("cores", i, u)
+        T[i, 0] = S[i, k, 0] + SR[i, 0]
+        for n, (_, at) in enumerate(plane):
+            start(
+                ("last", n),
+                copy(T.at[i, 0, at // 4, at % 4], RD.at[n], ld_s.at[n], ld_r.at[n], plane[n]),
+            )
+
+    def last2(i):
+        total = T[i, 0, x, y]
+        for n in range(15):
+            arrive("last", n)
+            total = total + RD[n]
+        rows_out[i, lax.rem(z + ORDER[0], 8)] = total
 
     stores = []
 
@@ -388,41 +414,52 @@
         store(grads.at[n], (gg, gu, gd)[n])
 
     pieces(0)
-    pl.semaphore_wait(barrier, 9)
-    gather1(0, 0)
+    pl.semaphore_wait(barrier, 18)
+    direct1(0, 0)
+    gather1(0, 1)
     swap_weights()
-    gather2(0, 0)
     pieces(1)
     gather1(1, 0)
-    gather1(0, 1)
+    gather1(1, 1)
+    gather2(0, 1)
+    expand_theirs()
+    direct2(0, 0)
     acc[...] = jnp.zeros_like(acc)
-    expand_theirs()
-    gather3(0, 0)
     gather2(1, 0)
-    gather2(0, 1)
-    gather1(1, 1)
-    gather4(0, 0, 0)
+    gather2(1, 1)
+    gather1(0, 2)
+    gather1(0, 3)
+    gather4(0, 0)
     step0(0)
     step0(1)
-    gather4(0, 0, 1)
+    gather3(0, 1)
     gather3(1, 0)
-    gather2(1, 1)
+    gather2(0, 2)
+    gather2(0, 3)
+    gather1(1, 2)
+    gather1(1, 3)
+    gather4(0, 1)
     step(0, 1)
     step(1, 1)
-    gather3(0, 1)
-    gather4(1, 0, 0)
+    gather4(1, 0)
     step0(2)
-    gather4(0, 1, 0)
-    gather4(0, 1, 1)
+    gather3(1, 1)
+    gather3(0, 2)
+    gather3(0, 3)
+    gather2(1, 2)
+    gather2(1, 3)
+    gather4(0, 2)
+    gather4(0, 3)
     step(0, 2)
     step(1, 2)
-    gather4(1, 0, 1)
+    gather4(1, 1)
     step(2, 1)
-    gather3(1, 1)
+    gather3(1, 2)
+    gather3(1, 3)
     step(0, 3)
     step(1, 3)
-    gather4(1, 1, 0)
-    gather4(1, 1, 1)
+    gather4(1, 2)
+    gather4(1, 3)
     step(2, 2)
     finish(0)
     finish(1)
@@ -469,23 +506,22 @@
     products(1, 3)
     grad(0, 0, 4)
     grad_swap(0)
-    scatter1(1, 3)
+    last1(1, 8)
     scatter2(1, 2)
     grad(1, 0, 4)
     grad_swap(1)
     scatter3(0, 0)
     scatter3(0, 1)
     scatter3(0, 2)
-    scatter2(1, 3)
     deliver(0)
     grad_end(2)
     scatter3(1, 0)
     scatter3(1, 1)
     grad_end(0)
     grad_end(1)
-    settle(8)
+    settle(18)
     scatter3(1, 2)
-    scatter3(1, 3)
+    last2(1)
     deliver(1)
     for c in stores:
         c.wait()
@@ -526,12 +562,13 @@
         V((2, BLOCK, BLOCK), F32),
         V((3, BLOCK, BLOCK), F32),
         V((3, 8, BLOCK, BLOCK), BF16),
-        V((2, 2, 4, 4, 8, 24, LANES), F32),
-        V((2, 4, 4, 8, 24, LANES), F32),
-        V((2, 4, 4, 8, 24, LANES), F32),
-        V((2, 3, 4, 8, 24, LANES), F32),
-        V((2, 4, 8, 24, LANES), F32),
+        V((2, 2, 8, 4, 4, 24, LANES), F32),
+        V((2, 8, 4, 4, 24, LANES), F32),
+        V((2, 8, 4, 4, 24, LANES), F32),
+        V((2, 3, 8, 4, 24, LANES), F32),
+        V((2, 8, 4, 24, LANES), F32),
         V((2, 3, 8, 24, LANES), F32),
+        V((15, 24, LANES), F32),
         V((3, 2, width, BLOCK), F32),
         V((3, width, BLOCK), BF16),
         V((3, width, BLOCK), BF16),
@@ -540,13 +577,15 @@
         V((2, width, n_tok), BF16),
         dma((5,)), dma((5,)),
         dma((3,)), dma((3,)),
-        dma((2, 2, 2, 2, 3)), dma((2, 2, 2, 2, 3)),
-        dma((2, 2, 2)), dma((2, 2, 2)),
+        dma((15,)), dma((15,)),
+        dma((2, 4, 2, 3)), dma((2, 4, 2, 3)),
+        dma((2, 4)), dma((2, 4)),
         dma((3, 2, 4)), dma((3, 2, 4)),
         dma((3, 2, 4)), dma((3, 2, 4)),
         dma((2, 10)), dma((2, 10)),
         dma((2, 10, 2, 3)), dma((2, 10, 2, 3)),
         dma((3,)), dma((3,)),
+        dma((15,)), dma((15,)),
     ]
     anywhere = pl.BlockSpec(memory_space=pl.ANY)
     held = pl.pallas_call(

time: 100 us -> 97.1 us (0.971)
  Pallas kernels: 99 us -> 96.4 us
    pallas_call x1, Pallas kernels: 97.1 us -> 94.4 us  [body(): pl.pallas_call(kernel, out_shape=shapes, in_specs=[anywhere] * 5, out_spe...]
where the time goes in v6:
time: 97.1 us; the launch traced here: 97 us
  Pallas kernels  96.4 us (99%)
    pallas_call x1, Pallas kernels, body(): pl.pallas_call(kernel, out_shape=shapes, in_specs=[anywhere] * 5, out_spe...  94.4 us

profile of v6, /device:TPU:1, one launch (start us, length us, event | category | flops | bytes accessed | tf_op | source)
XLA Modules:
  0.0 97.0 jit_solution(9616846180028843112)
XLA Ops:
  0.6 94.4 %feed_forward.1 = (bf16[192,128]{1,0:T(8,128)(2,1)}, bf16[192,128]{1,0:T(8,128)(2,1)}, bf16[192,512]{1,0:T(8,128)(2,1)}, bf16[192,512]{1,0:T(8,128)(2,1)}, bf16[192,512]{1,0:T(8,128)(2,1)}) custom-call(bf16[192,128]{1,0:T(8,128)(2,1)} %bitcast.7, bf16[192,512]{1,0:T(8,128)(2,1)} %gw.1, bf16[192,512]{1,0:T(8,128)(2,1)} %uw.1, bf16[192,512]{1,0:T(8,128)(2,1)} %bitcast.6, ...), custom_call_target="tpu_custom_call" | custom-call | tf_op jit(solution)/shard_map/feed_forward/pallas_call | solution.py:591
  95.1 1.9 %hand_over.1 = (bf16[192,128]{1,0:T(8,128)(2,1)}, bf16[192,128]{1,0:T(8,128)(2,1)}, bf16[192,512]{1,0:T(8,128)(2,1)}, bf16[192,512]{1,0:T(8,128)(2,1)}, bf16[192,512]{1,0:T(8,128)(2,1)}) custom-call(bf16[192,128]{1,0:T(8,128)(2,1)} %get-tuple-element.15.refs_0_, bf16[192,128]{1,0:T(8,128)(2,1)} %get-tuple-element.16.refs_1_, ...), custom_call_target="tpu_custom_call" | custom-call | tf_op jit(solution)/shard_map/hand_over/pallas_call | solution.py:602

commit v7 on v6

--- a/solution.py
+++ b/solution.py
@@ -417,37 +417,37 @@
     pl.semaphore_wait(barrier, 18)
     direct1(0, 0)
     gather1(0, 1)
+    gather1(0, 2)
+    gather1(0, 3)
     swap_weights()
     pieces(1)
     gather1(1, 0)
     gather1(1, 1)
     gather2(0, 1)
+    gather2(1, 0)
     expand_theirs()
     direct2(0, 0)
+    gather2(0, 2)
+    gather2(0, 3)
+    gather2(1, 1)
+    gather1(1, 2)
+    gather1(1, 3)
     acc[...] = jnp.zeros_like(acc)
-    gather2(1, 0)
-    gather2(1, 1)
-    gather1(0, 2)
-    gather1(0, 3)
+    gather3(0, 1)
     gather4(0, 0)
     step0(0)
     step0(1)
-    gather3(0, 1)
     gather3(1, 0)
-    gather2(0, 2)
-    gather2(0, 3)
-    gather1(1, 2)
-    gather1(1, 3)
     gather4(0, 1)
     step(0, 1)
     step(1, 1)
-    gather4(1, 0)
-    step0(2)
-    gather3(1, 1)
     gather3(0, 2)
     gather3(0, 3)
     gather2(1, 2)
     gather2(1, 3)
+    gather4(1, 0)
+    step0(2)
+    gather3(1, 1)
     gather4(0, 2)
     gather4(0, 3)
     step(0, 2)
@@ -474,32 +474,30 @@
     relay_step(0, 2)
     products(0, 0)
     relay_step(1, 1)
-    scatter1(0, 0)
     relay_step(2, 1)
     products(1, 0)
-    grad(2, 2, 4)
+    scatter1(0, 0)
     relay_step(0, 3)
     products(0, 1)
+    grad(2, 2, 4)
+    relay_step(1, 2)
     scatter1(1, 0)
+    relay_step(2, 2)
     scatter2(0, 0)
-    relay_step(1, 2)
+    products(1, 1)
     scatter1(0, 1)
-    relay_step(2, 2)
-    products(1, 1)
-    scatter2(1, 0)
     relay_end(0)
     products(0, 2)
-    scatter1(1, 1)
     grad(2, 0, 2)
     grad_swap(2)
+    relay_step(1, 3)
+    scatter2(1, 0)
+    scatter1(1, 1)
     scatter1(0, 2)
-    relay_step(1, 3)
+    relay_step(2, 3)
+    products(1, 2)
+    settle(24)
     scatter2(0, 1)
-    relay_step(2, 3)
-    settle(24)
-    products(1, 2)
-    scatter2(1, 1)
-    scatter2(0, 2)
     scatter1(1, 2)
     relay_end(1)
     relay_end(2)
@@ -507,6 +505,8 @@
     grad(0, 0, 4)
     grad_swap(0)
     last1(1, 8)
+    scatter2(1, 1)
+    scatter2(0, 2)
     scatter2(1, 2)
     grad(1, 0, 4)
     grad_swap(1)

time: 97.1 us -> 100 us (1.030)
  Pallas kernels: 96.4 us -> 99.2 us
    pallas_call x1, Pallas kernels: 94.4 us -> 97.3 us  [body(): pl.pallas_call(kernel, out_shape=shapes, in_specs=[anywhere] * 5, out_spe...]
where the time goes in v7:
time: 100 us; the launch traced here: 99.8 us
  Pallas kernels  99.2 us (99%)
    pallas_call x1, Pallas kernels, body(): pl.pallas_call(kernel, out_shape=shapes, in_specs=[anywhere] * 5, out_spe...  97.3 us

profile of v7, /device:TPU:1, one launch (start us, length us, event | category | flops | bytes accessed | tf_op | source)
XLA Modules:
  0.0 99.8 jit_solution(12336579521229777286)
XLA Ops:
  0.6 97.3 %feed_forward.1 = (bf16[192,128]{1,0:T(8,128)(2,1)}, bf16[192,128]{1,0:T(8,128)(2,1)}, bf16[192,512]{1,0:T(8,128)(2,1)}, bf16[192,512]{1,0:T(8,128)(2,1)}, bf16[192,512]{1,0:T(8,128)(2,1)}) custom-call(bf16[192,128]{1,0:T(8,128)(2,1)} %bitcast.7, bf16[192,512]{1,0:T(8,128)(2,1)} %gw.1, bf16[192,512]{1,0:T(8,128)(2,1)} %uw.1, bf16[192,512]{1,0:T(8,128)(2,1)} %bitcast.6, ...), custom_call_target="tpu_custom_call" | custom-call | tf_op jit(solution)/shard_map/feed_forward/pallas_call | solution.py:591
  97.9 1.9 %hand_over.1 = (bf16[192,128]{1,0:T(8,128)(2,1)}, bf16[192,128]{1,0:T(8,128)(2,1)}, bf16[192,512]{1,0:T(8,128)(2,1)}, bf16[192,512]{1,0:T(8,128)(2,1)}, bf16[192,512]{1,0:T(8,128)(2,1)}) custom-call(bf16[192,128]{1,0:T(8,128)(2,1)} %get-tuple-element.15.refs_0_, bf16[192,128]{1,0:T(8,128)(2,1)} %get-tuple-element.16.refs_1_, ...), custom_call_target="tpu_custom_call" | custom-call | tf_op jit(solution)/shard_map/hand_over/pallas_call | solution.py:602

commit v8 on v6

--- a/solution.py
+++ b/solution.py
@@ -46,7 +46,7 @@
 def kernel(
     tok, gw, uw, dw, cot,
     out, gt, gg, gu, gd,
-    acts, weights, rows_in, X, W, WE, WP, sent, got, part, final, H,
+    acts, weights, rows_in, X, W, WE, WP, sent, got, part, ahead, final, H,
     S, SR, T, RX, U, RY, RD, acc, gsend, ggot, grads, rows_out, results,
     in_s, out_s, w_s, w_r, di_s, di_r, ag_s, ag_r, fw_s, fw_r, rs_s, rs_r, ga_s, ga_r, sx_s, sx_r, xy_s, xy_r, gr_s, gr_r, ld_s, ld_r,
 ):
@@ -61,7 +61,8 @@
     xpeers = {i: (row, lax.rem(x + i, 4) * 4 + y) for i in (1, 2, 3)}
     ypeers = {i: (row, x * 4 + lax.rem(y + i, 4)) for i in (1, 2, 3)}
     peers = (xpeers, ypeers)
-    plane = [(row, lax.rem(x + i, 4) * 4 + lax.rem(y + j, 4)) for i in range(4) for j in range(4)][1:]
+    hops = sorted(((i, j) for i in range(4) for j in range(4)), key=lambda v: -(min(v[0], 4 - v[0]) + min(v[1], 4 - v[1])))
+    plane = [(row, lax.rem(x + i, 4) * 4 + lax.rem(y + j, 4)) for i, j in hops[:15]]
 
     def copy(src, dst, s, r, device):
         return pltpu.make_async_remote_copy(
@@ -84,10 +85,6 @@
             if key not in sent_off:
                 started[key].wait_send()
                 sent_off.append(key)
-
-    barrier = pltpu.get_barrier_semaphore()
-    for device in [sibling, right, left, *plane]:
-        pl.semaphore_signal(barrier, inc=1, device_id=device, device_id_type=MESH)
 
     first_half = lax.broadcasted_iota(jnp.int32, (PIECE, LANES), 1) < TAIL
     loads = [
@@ -99,19 +96,24 @@
     for c in loads:
         c.start()
 
+    barrier = pltpu.get_barrier_semaphore()
+    for device in [sibling, right, left, *plane]:
+        pl.semaphore_signal(barrier, inc=1, device_id=device, device_id_type=MESH)
+
     def pieces(a):
         loads[a].wait()
         one = identity(HALF)
         tails = acts[a, pl.ds(LANES, TAIL), :]
         rows_in[a, 0] = dot(one, acts[a, pl.ds(0, LANES), :], 1, 1)
         rows_in[a, 1] = dot(one, jnp.concatenate([tails, tails], axis=0), 1, 1)
-        for q in range(4):
-            at = [pl.ds(pl.multiple_of(lax.rem(z + ORDER[2 * q + e], 8) * PIECE, PIECE), PIECE) for e in range(2)]
-            for e in range(2):
-                X[a, k, q, x, y, pl.ds(e * PIECE, PIECE), :] = rows_in[a, 0, at[e], :].astype(BF16)
-            X[a, k, q, x, y, pl.ds(2 * PIECE, PIECE), :] = jnp.where(
-                first_half, rows_in[a, 1, at[0], :], rows_in[a, 1, at[1], :]
-            ).astype(BF16)
+
+    def piece(a, q):
+        at = [pl.ds(pl.multiple_of(lax.rem(z + ORDER[2 * q + e], 8) * PIECE, PIECE), PIECE) for e in range(2)]
+        for e in range(2):
+            X[a, k, q, x, y, pl.ds(e * PIECE, PIECE), :] = rows_in[a, 0, at[e], :].astype(BF16)
+        X[a, k, q, x, y, pl.ds(2 * PIECE, PIECE), :] = jnp.where(
+            first_half, rows_in[a, 1, at[0], :], rows_in[a, 1, at[1], :]
+        ).astype(BF16)
 
     def direct1(a, q):
         ref = X.at[a, k, q, x, y]
@@ -196,14 +198,15 @@
     def half(dr):
         return pl.ds(HALF * dr, HALF)
 
-    def chain(a, dr, s, rows):
+    def chain(a, dr, s, rows, sem=None):
+        sem = s if sem is None else sem
         start(
-            ("chain", a, dr, s),
+            ("chain", a, dr, sem),
             copy(
                 sent.at[a, dr, s, rows],
                 got.at[a, dr, s, rows],
-                rs_s.at[a, dr, s],
-                rs_r.at[a, dr, s],
+                rs_s.at[a, dr, sem],
+                rs_r.at[a, dr, sem],
                 (right, left)[dr],
             ),
         )
@@ -218,12 +221,22 @@
             part[dr] = local(a, PLACE[(4 - s, 4 + s)[dr]], 0, BLOCK)
         for dr in range(2):
             arrive("chain", a, dr, s - 1)
-            if s == 1:
-                sent[a, dr, s, half(dr), :] = (part[dr, half(dr), :] + got[a, dr, 0, half(dr), :].astype(F32)).astype(BF16)
-                sent[a, dr, s, half(1 - dr), :] = part[dr, half(1 - dr), :].astype(BF16)
-            else:
-                sent[a, dr, s] = (part[dr] + got[a, dr, s - 1].astype(F32)).astype(BF16)
+            if s == 2:
+                arrive("chain", a, dr, 4)
+            sent[a, dr, s] = (part[dr] + got[a, dr, s - 1].astype(F32)).astype(BF16)
             chain(a, dr, s, pl.ds(0, BLOCK))
+
+    def step1a(a):
+        for dr in range(2):
+            ahead[a, dr] = local(a, PLACE[(3, 5)[dr]], 2 * dr, HALF)
+            sent[a, dr, 1, half(1 - dr), :] = local(a, PLACE[(3, 5)[dr]], 2 - 2 * dr, HALF).astype(BF16)
+            chain(a, dr, 1, half(1 - dr), 4)
+
+    def step1b(a):
+        for dr in range(2):
+            arrive("chain", a, dr, 0)
+            sent[a, dr, 1, half(dr), :] = (ahead[a, dr] + got[a, dr, 0, half(dr), :].astype(F32)).astype(BF16)
+            chain(a, dr, 1, half(dr))
 
     def finish(a):
         final[a] = local(a, PLACE[0], 0, BLOCK)
@@ -234,19 +247,27 @@
     def relay_step(m, s):
         for dr in range(2):
             places = (RIGHTWARD, LEFTWARD)[dr]
-            rows = half(dr) if s == 3 else pl.ds(0, BLOCK)
             if s > 0:
                 arrive("relay", m, dr, s - 1)
-            start(
-                ("relay", m, dr, s),
-                copy(
-                    H.at[m, places[s], rows],
-                    H.at[m, places[s + 1], rows],
-                    ga_s.at[m, dr, s],
-                    ga_r.at[m, dr, s],
-                    (right, left)[dr],
-                ),
-            )
+            parts = [(s, pl.ds(0, BLOCK))]
+            if s == 3 or (s == 2 and m > 0):
+                parts = [(s, half(dr)), (4, half(1 - dr))][: 4 - s]
+            for sem, rows in parts:
+                start(
+                    ("relay", m, dr, sem),
+                    copy(
+                        H.at[m, places[s], rows],
+                        H.at[m, places[s + 1], rows],
+                        ga_s.at[m, dr, sem],
+                        ga_r.at[m, dr, sem],
+                        (right, left)[dr],
+                    ),
+                )
+
+    def relay_rest():
+        for m in (1, 2):
+            for dr in range(2):
+                arrive("relay", m, dr, 4)
 
     def relay_end(m):
         for dr in range(2):
@@ -353,6 +374,20 @@
             for p in range(n):
                 rows_out[i, lax.rem(z + ORDER[lo + p], 8), rows, :] = total[p]
 
+    def last_product(step):
+        for h in (other, k):
+            p = dot(H[1 + step, 0], WP[step, h], 1, 1)
+            if step == 0:
+                part[h] = p
+                continue
+            p += part[h]
+            S[1, h, 0, :, :, pl.ds(0, PIECE), :] = p[:, :LANES].reshape(4, 4, PIECE, LANES)
+            tail = p[:, LANES:].reshape(4, 4, PIECE, LANES)
+            low = lax.broadcasted_iota(jnp.int32, (4, 4, 8, LANES), 3) < TAIL
+            S[1, h, 0, :, :, pl.ds(PIECE, 8), :] = jnp.where(low, tail[:, :, :8], tail[:, :, 8:])
+            if h is other:
+                start(("cores", 1, 8), copy(S.at[1, other, 0], SR.at[1, 0], sx_s.at[1, 8], sx_r.at[1, 8], sibling))
+
     def last1(i, u):
         arrive("cores", i, u)
         T[i, 0] = S[i, k, 0] + SR[i, 0]
@@ -414,11 +449,16 @@
         store(grads.at[n], (gg, gu, gd)[n])
 
     pieces(0)
+    piece(0, 0)
     pl.semaphore_wait(barrier, 18)
     direct1(0, 0)
+    for q in (1, 2, 3):
+        piece(0, q)
     gather1(0, 1)
     swap_weights()
     pieces(1)
+    for q in range(4):
+        piece(1, q)
     gather1(1, 0)
     gather1(1, 1)
     gather2(0, 1)
@@ -434,13 +474,15 @@
     step0(1)
     gather3(0, 1)
     gather3(1, 0)
+    gather4(0, 1)
+    step1a(0)
+    step1a(1)
     gather2(0, 2)
     gather2(0, 3)
     gather1(1, 2)
     gather1(1, 3)
-    gather4(0, 1)
-    step(0, 1)
-    step(1, 1)
+    step1b(0)
+    step1b(1)
     gather4(1, 0)
     step0(2)
     gather3(1, 1)
@@ -453,7 +495,8 @@
     step(0, 2)
     step(1, 2)
     gather4(1, 1)
-    step(2, 1)
+    step1a(2)
+    step1b(2)
     gather3(1, 2)
     gather3(1, 3)
     step(0, 3)
@@ -497,13 +540,15 @@
     scatter2(0, 1)
     relay_step(2, 3)
     settle(24)
+    relay_rest()
     products(1, 2)
     scatter2(1, 1)
     scatter2(0, 2)
     scatter1(1, 2)
     relay_end(1)
+    last_product(0)
     relay_end(2)
-    products(1, 3)
+    last_product(1)
     grad(0, 0, 4)
     grad_swap(0)
     last1(1, 8)
@@ -560,6 +605,7 @@
         V((3, 2, 4, BLOCK, BLOCK), BF16),
         V((3, 2, 4, BLOCK, BLOCK), BF16),
         V((2, BLOCK, BLOCK), F32),
+        V((3, 2, HALF, BLOCK), F32),
         V((3, BLOCK, BLOCK), F32),
         V((3, 8, BLOCK, BLOCK), BF16),
         V((2, 2, 8, 4, 4, 24, LANES), F32),
@@ -580,8 +626,8 @@
         dma((15,)), dma((15,)),
         dma((2, 4, 2, 3)), dma((2, 4, 2, 3)),
         dma((2, 4)), dma((2, 4)),
-        dma((3, 2, 4)), dma((3, 2, 4)),
-        dma((3, 2, 4)), dma((3, 2, 4)),
+        dma((3, 2, 5)), dma((3, 2, 5)),
+        dma((3, 2, 5)), dma((3, 2, 5)),
         dma((2, 10)), dma((2, 10)),
         dma((2, 10, 2, 3)), dma((2, 10, 2, 3)),
         dma((3,)), dma((3,)),

time: 97.1 us -> 97 us (level)
  no operation moved by 1% of the time
where the time goes in v8:
time: 97 us; the launch traced here: 96.8 us
  Pallas kernels  96.2 us (99%)
    pallas_call x1, Pallas kernels, body(): pl.pallas_call(kernel, out_shape=shapes, in_specs=[anywhere] * 5, out_spe...  94.2 us

profile of v8, /device:TPU:1, one launch (start us, length us, event | category | flops | bytes accessed | tf_op | source)
XLA Modules:
  0.0 96.8 jit_solution(16547844274275651059)
XLA Ops:
  0.6 94.2 %feed_forward.1 = (bf16[192,128]{1,0:T(8,128)(2,1)}, bf16[192,128]{1,0:T(8,128)(2,1)}, bf16[192,512]{1,0:T(8,128)(2,1)}, bf16[192,512]{1,0:T(8,128)(2,1)}, bf16[192,512]{1,0:T(8,128)(2,1)}) custom-call(bf16[192,128]{1,0:T(8,128)(2,1)} %bitcast.7, bf16[192,512]{1,0:T(8,128)(2,1)} %gw.1, bf16[192,512]{1,0:T(8,128)(2,1)} %uw.1, bf16[192,512]{1,0:T(8,128)(2,1)} %bitcast.6, ...), custom_call_target="tpu_custom_call" | custom-call | tf_op jit(solution)/shard_map/feed_forward/pallas_call | solution.py:637
  94.9 1.9 %hand_over.1 = (bf16[192,128]{1,0:T(8,128)(2,1)}, bf16[192,128]{1,0:T(8,128)(2,1)}, bf16[192,512]{1,0:T(8,128)(2,1)}, bf16[192,512]{1,0:T(8,128)(2,1)}, bf16[192,512]{1,0:T(8,128)(2,1)}) custom-call(bf16[192,128]{1,0:T(8,128)(2,1)} %get-tuple-element.15.refs_0_, bf16[192,128]{1,0:T(8,128)(2,1)} %get-tuple-element.16.refs_1_, ...), custom_call_target="tpu_custom_call" | custom-call | tf_op jit(solution)/shard_map/hand_over/pallas_call | solution.py:648
